TPU v7x, 256 devices: a whole 4x4x8 slice. The times are simulated.
256 devices in a mesh: dp: 32 (over y, z), mp: 8 (over x, core).
Axes of the slice: x: 4, y: 4, z: 8, core: 2. Of those that a mesh axis runs over, the one named last changes fastest.
Arguments:
- features: bfloat16 [4096, 4096], P('dp'), may hold values from -6 to 6
- upstream: bfloat16 [4096, 8192], P('dp', 'mp'), may hold values from -0.25 to 0.25
- stats: float32 [32, 8, 512, 512], P('dp', 'mp'), may hold values from -0.5 to 1024000, as said below
- accum: float32 [4096, 8192], P('dp', 'mp'), may hold values from 0.01 to 600, as said below
Outputs:
- new_stats: float32 [32, 8, 512, 512], P('dp', 'mp')
- new_accum: float32 [4096, 8192], P('dp', 'mp')
- update: bfloat16 [4096, 8192], P(None, 'mp')
Inputs may be any that keep to these rules, and one draw needn't show every extreme that they name: Each stats[i, g] is symmetric; its diagonal entries are at least 512 and exceed the sum of magnitudes of the other entries of their row. `accum`: every entry is positive.
All inputs are finite; a program needn't handle non-finite values.
Results may differ from a plain program's by a relative error of at most 0.0006.
Values may be sent and summed in bfloat16 or wider, within the bound.
A program may use at most 128 MiB of HBM per device.

v0:
```python
import jax
import jax.numpy as jnp
from jax import lax
from jax.sharding import PartitionSpec as P

ITERS = 6


def from_partner(x, axis, distance):
    return lax.ppermute(x, axis, [(i, i ^ 1 << distance) for i in range(lax.axis_size(axis))])


def product(first, second):
    return jnp.dot(
        first, second, precision=lax.Precision.HIGHEST, preferred_element_type=jnp.float32
    )


def newton_root(stat):
    identity = jnp.eye(stat.shape[-1], dtype=jnp.float32)
    factor = 2.5 / jnp.sqrt(jnp.sum(stat * stat, axis=(-2, -1), keepdims=True))
    iterate = identity * factor**0.25
    coupled = stat * factor
    for iteration in range(ITERS):
        step_factor = (5.0 * identity - coupled) * 0.25
        iterate = product(iterate, step_factor)
        if iteration + 1 < ITERS:
            squared = product(step_factor, step_factor)
            coupled = product(squared, product(squared, coupled))
    return iterate


def shards(features, upstream, stats, accum):
    feature_cols = features.shape[1]
    owners = lax.axis_size("dp")
    own_rows = feature_cols // owners
    block_size = 4 * own_rows
    gradient = lax.psum_scatter(
        lax.dot_general(
            features, upstream, (((0,), (0,)), ((), ())), preferred_element_type=jnp.float32
        ),
        "dp",
        scatter_dimension=0,
        tiled=True,
    )
    new_accum = accum + gradient * gradient
    adagrad = gradient / jnp.sqrt(new_accum)
    member = lax.axis_index("dp") % 4
    my_side = member % 2
    column = member // 2
    partner_rows = from_partner(gradient, "dp", 0)
    lower_half = my_side == 0
    pair_block = jnp.where(
        lower_half,
        jnp.concatenate([gradient, partner_rows], 0),
        jnp.concatenate([partner_rows, gradient], 0),
    )
    other_rows = from_partner(pair_block, "dp", 1)
    quad_block = jnp.where(
        member < 2,
        jnp.concatenate([pair_block, other_rows], 0),
        jnp.concatenate([other_rows, pair_block], 0),
    )
    my_block = lax.dynamic_slice_in_dim(quad_block, column * block_size, block_size, 1)
    operand = jnp.where(lower_half, my_block, my_block.T)
    new_stat = stats[0, 0] + product(operand, operand.T)
    my_root = newton_root(new_stat)
    partner_root = from_partner(my_root, "dp", 0)
    far_roots = from_partner((my_root, partner_root), "dp", 1)

    def root_of(target):
        near = jnp.where(member == target, my_root, partner_root)
        far = jnp.where(member ^ 2 == target, far_roots[0], far_roots[1])
        return jnp.where(member // 2 == target // 2, near, far)

    pieces = []
    for half_index in range(2):
        left_root = root_of(2 * half_index)
        right_root = root_of(2 * half_index + 1)
        block_cols = quad_block[:, half_index * block_size : (half_index + 1) * block_size]
        left_rows = lax.dynamic_slice_in_dim(left_root, member * own_rows, own_rows, 0)
        pieces.append(product(product(left_rows, block_cols), right_root))
    precond = jnp.concatenate(pieces, 1)
    precond_local = jnp.sum(precond * precond)
    adagrad_total, precond_total = lax.psum(
        (jnp.sum(adagrad * adagrad), precond_local), ("dp", "mp")
    )
    scaled = (precond * jnp.sqrt(adagrad_total / (precond_total + 1e-12))).astype(jnp.bfloat16)
    update = lax.all_gather(scaled, "dp", axis=0, tiled=True)
    return (new_stat[None, None], new_accum, update)


def solution(mesh):
    placed = (P("dp", None), P("dp", "mp"), P("dp", "mp", None, None), P("dp", "mp"))
    return jax.shard_map(
        shards,
        mesh=mesh,
        in_specs=placed,
        out_specs=(P("dp", "mp", None, None), P("dp", "mp"), P(None, "mp")),
        check_vma=False,
    )
```

profile of v0, /device:TPU:32, one launch (start us, length us, event | category | flops | bytes accessed | tf_op | source)
XLA Modules:
  0.0 659.3 jit_solution(14257335789425289478)
XLA Ops:
  7.2 0.0 copy-start
  7.2 0.0 reduce-scatter.2.cloned.1.call-start
  7.2 1.2 copy-done
  8.4 9.0 %fusion.134 = f32[4096,1024]{1,0:T(8,128)} fusion(bf16[128,4096]{1,0:T(8,128)(2,1)S(1)} %copy-done, bf16[128,1024]{1,0:T(8,128)(2,1)} %param.5), kind=kOutput, calls=%fused_computation.142 | convolution fusion | flops 1073741824 | bytes 18087936 | tf_op jit(solution)/shard_map/dot_general | solution.py:39
  17.4 0.0 reduce-scatter.2.cloned.1.call-update
  17.5 0.0 all-gather.2.cloned.1.call-start
  17.5 247.0 %reduce-scatter.2.cloned.1.call-done = f32[128,1024]{1,0:T(8,128)} async-done(((f32[4096,1024]{1,0:T(8,128)}), f32[128,1024]{1,0:T(8,128)}) %reduce-scatter.2.cloned.1.call-update) | async-done | bytes 524304 | tf_op jit(solution)/shard_map/reduce_scatter | solution.py:38
  264.5 1.1 collective-permute-start
  265.6 8.6 %collective-permute-done = f32[128,1024]{1,0:T(8,128)S(1)} collective-permute-done((f32[128,1024]{1,0:T(8,128)}, f32[128,1024]{1,0:T(8,128)S(1)}, u32[]{:S(2)}, u32[]{:S(2)}) %collective-permute-start) | collective-permute-done | bytes 524320 | tf_op jit(solution)/shard_map/ppermute | solution.py:10
  274.2 1.4 maximum_select_fusion.1
  275.6 2.9 collective-permute-start.1
  278.5 40.2 %collective-permute-done.1 = f32[256,1024]{1,0:T(8,128)} collective-permute-done((f32[256,1024]{1,0:T(8,128)S(1)}, f32[256,1024]{1,0:T(8,128)}, u32[]{:S(2)}, u32[]{:S(2)}) %collective-permute-start.1) | collective-permute-done | bytes 1048608 | tf_op jit(solution)/shard_map/ppermute | solution.py:10
  318.7 1.9 maximum_select_fusion
  320.5 0.1 constant_dynamic-slice_fusion
  320.6 1.3 copy.7
  321.9 5.3 multiply_reduce_fusion
  327.3 0.0 copy-start.2
  328.1 3.7 fusion.38
  331.8 0.0 copy-done.2
  331.8 1.9 fusion.18
  333.7 1.9 fusion.20
  335.5 1.8 fusion.135
  337.4 1.9 fusion.34
  339.3 2.1 fusion.36
  341.4 1.8 fusion.136
  343.3 1.8 fusion.137
  345.1 1.9 fusion.30
  347.1 1.9 fusion.32
  349.0 1.8 fusion.138
  350.8 1.8 fusion.139
  352.7 2.1 fusion.26
  354.8 1.9 fusion.28
  356.7 1.8 fusion.140
  358.6 1.8 fusion.141
  360.5 1.9 fusion.22
  362.4 1.9 fusion.24
  364.3 1.8 fusion.142
  366.2 2.1 fusion
  368.3 1.8 fusion.143
  370.1 1.9 collective-permute-start.2
  372.0 1.8 collective-permute-start.3
  373.8 41.5 %collective-permute-done.2 = f32[512,512]{1,0:T(8,128)} collective-permute-done((f32[512,512]{1,0:T(8,128)S(1)}, f32[512,512]{1,0:T(8,128)}, u32[]{:S(2)}, u32[]{:S(2)}) %collective-permute-start.2) | collective-permute-done | bytes 1048608 | tf_op jit(solution)/shard_map/ppermute | solution.py:10
  415.4 3.9 collective-permute-start.4
  419.3 2.7 multiply_reduce_fusion.2
  422.0 20.3 %collective-permute-done.3 = f32[512,512]{1,0:T(8,128)} collective-permute-done((f32[512,512]{1,0:T(8,128)S(1)}, f32[512,512]{1,0:T(8,128)}, u32[]{:S(2)}, u32[]{:S(2)}) %collective-permute-start.3) | collective-permute-done | bytes 1048608 | tf_op jit(solution)/shard_map/ppermute | solution.py:10
  442.3 21.6 %collective-permute-done.4 = f32[512,512]{1,0:T(8,128)} collective-permute-done((f32[512,512]{1,0:T(8,128)}, f32[512,512]{1,0:T(8,128)}, u32[]{:S(2)}, u32[]{:S(2)}) %collective-permute-start.4) | collective-permute-done | bytes 1048608 | tf_op jit(solution)/shard_map/ppermute | solution.py:10
  464.0 1.8 fusion.6
  465.8 1.8 fusion.8
  467.7 2.1 fusion.14
  469.8 2.4 fusion.10
  472.1 0.8 multiply_reduce_fusion.1
  472.9 77.1 %all-reduce = (f32[]{:T(128)}, f32[]{:T(128)}) all-reduce(f32[]{:T(128)} %get-tuple-element.5, f32[]{:T(128)} %multiply_reduce_fusion.1), channel_id=1, replica_groups=mesh['dp'=32,'mp'=8] {'dp','mp'}, use_global_device_ids=true, to_apply=%region_3.4 | all-reduce | flops 2 | bytes 16 | tf_op jit(solution)/shard_map/psum | solution.py:85
  551.4 0.7 multiply_convert_fusion
  552.2 0.0 all-gather.2.cloned.1.call-update
  552.2 92.0 %all-gather.2.cloned.1.call-done = bf16[4096,1024]{1,0:T(8,128)(2,1)} async-done(((bf16[128,1024]{1,0:T(8,128)(2,1)}), bf16[4096,1024]{1,0:T(8,128)(2,1)}) %all-gather.2.cloned.1.call-update) | async-done | bytes 8388624 | tf_op jit(solution)/shard_map/all_gather | solution.py:89
  644.2 0.0 copy-start.1
  644.2 7.8 %copy.9 = bf16[4096,1024]{1,0:T(8,128)(2,1)} copy(bf16[4096,1024]{1,0:T(8,128)(2,1)} %all-gather.2.cloned.1.call-done) | data formatting | bytes 16777216
  652.0 0.0 copy-done.1
Async XLA Ops:
  7.2 1.2 copy-start
  7.2 257.3 %reduce-scatter.2.cloned.1.call-start = ((), (), s32[]{:S(2)}) async-start(), calls=%async_computation.1 | async-start | bytes 17301504 | tf_op jit(solution)/shard_map/reduce_scatter | solution.py:38
  17.5 626.7 %all-gather.2.cloned.1.call-start = ((), (), s32[]{:S(2)}) async-start(), calls=%async_computation.2 | async-start | bytes 8650752 | tf_op jit(solution)/shard_map/all_gather | solution.py:89
  264.5 9.7 %collective-permute-start = (f32[128,1024]{1,0:T(8,128)}, f32[128,1024]{1,0:T(8,128)S(1)}, u32[]{:S(2)}, u32[]{:S(2)}) collective-permute-start(f32[128,1024]{1,0:T(8,128)} %reduce-scatter.2.cloned.1.call-done), channel_id=1, source_target_pairs={{0,8},{8,0},{16,24},{24,16},{32,40},{40,32},{48,56},{56,48},{64,72... | collective-permute-start | bytes 1572872 | tf_op jit(solution)/shard_map/ppermute | solution.py:10
  275.6 43.1 %collective-permute-start.1 = (f32[256,1024]{1,0:T(8,128)S(1)}, f32[256,1024]{1,0:T(8,128)}, u32[]{:S(2)}, u32[]{:S(2)}) collective-permute-start(f32[256,1024]{1,0:T(8,128)S(1)} %maximum_select_fusion.1), channel_id=1, source_target_pairs={{0,16},{8,24},{16,0},{24,8},{32,48},{40,56},{48,32},{56,40},{64,80... | collective-permute-start | bytes 3145736 | tf_op jit(solution)/shard_map/ppermute | solution.py:10
  327.3 4.5 copy-start.2
  370.1 45.2 %collective-permute-start.2 = (f32[512,512]{1,0:T(8,128)S(1)}, f32[512,512]{1,0:T(8,128)}, u32[]{:S(2)}, u32[]{:S(2)}) collective-permute-start(f32[512,512]{1,0:T(8,128)S(1)} %fusion.143), channel_id=1, source_target_pairs={{0,8},{8,0},{16,24},{24,16},{32,40},{40,32},{48,56},{56,48},{64,72... | collective-permute-start | bytes 3145736 | tf_op jit(solution)/shard_map/ppermute | solution.py:10
  372.0 70.3 %collective-permute-start.3 = (f32[512,512]{1,0:T(8,128)S(1)}, f32[512,512]{1,0:T(8,128)}, u32[]{:S(2)}, u32[]{:S(2)}) collective-permute-start(f32[512,512]{1,0:T(8,128)S(1)} %fusion.143), channel_id=1, source_target_pairs={{0,16},{8,24},{16,0},{24,8},{32,48},{40,56},{48,32},{56,40},{64,80... | collective-permute-start | bytes 3145736 | tf_op jit(solution)/shard_map/ppermute | solution.py:10
  415.4 48.6 %collective-permute-start.4 = (f32[512,512]{1,0:T(8,128)}, f32[512,512]{1,0:T(8,128)}, u32[]{:S(2)}, u32[]{:S(2)}) collective-permute-start(f32[512,512]{1,0:T(8,128)} %collective-permute-done.2), channel_id=1, source_target_pairs={{0,16},{8,24},{16,0},{24,8},{32,48},{40,56},{48,32},{56,40},{64,80... | collective-permute-start | bytes 3145736 | tf_op jit(solution)/shard_map/ppermute | solution.py:10
  644.2 7.8 %copy-start.1 = (bf16[128,4096]{1,0:T(8,128)(2,1)S(1)}, bf16[128,4096]{1,0:T(8,128)(2,1)}, u32[]{:S(2)}) copy-start(bf16[128,4096]{1,0:T(8,128)(2,1)} %param.4) | copy-start | bytes 3145732
Sparse Core Ops, SparseCore 0:
  17.6 246.8 reduce-scatter.1
  552.3 91.8 all-gather.1
where the time goes:
time: 665 us; the launch traced here: 659 us
  waiting for transfers between devices  471 us (71%)
  blocking collectives  77.1 us (12%)
  matrix products  64.4 us (10%)
  between operations  16.9 us (3%)
  starting transfers between devices  11.7 us (2%)
  local copies, waits for them, and re-layouts  10.4 us (2%)
  other arithmetic  7.48 us (1%)
    reduce_scatter x1, waiting for transfers between devices, shards(): lax.psum_scatter(lax.dot_general(features, upstream, (((0,), (0,)), ((),...  247 us
    ppermute x5, waiting for transfers between devices, from_partner(): lax.ppermute(x, axis, [(i, i ^ 1 << distance) for i in range(lax.axis_siz...  132 us
    all_gather x1, waiting for transfers between devices, shards(): update = lax.all_gather(scaled, 'dp', axis=0, tiled=True)  92 us
    psum x1, blocking collectives, shards(): lax.psum((jnp.sum(adagrad * adagrad), precond_local), ('dp', 'mp'))  77.1 us
    dot_general x26, matrix products, product(): jnp.dot(first, second, precision=lax.Precision.HIGHEST, preferred_element...  55.3 us
  transfers between devices with their start and end apart: 7, of which 7 were waited for; matrix products, arithmetic and copies ran while one was open for 0% of the time, Pallas kernels for 0%

commit v1 on v0

v1 whole, which is shorter than its diff:
```python
import functools

import jax
import jax.numpy as jnp
from jax import lax
from jax.experimental import pallas as pl
from jax.experimental.pallas import tpu as pltpu
from jax.sharding import PartitionSpec as P

ITERS = 6
NX, NY, NZ, NC = 4, 4, 8, 2
MESH = pl.DeviceIdType.MESH
BLOCK = 512
HALF = BLOCK // 2
ROWS_A = 96
ROWS_B = HALF - ROWS_A


def place():
    dp, mp = lax.axis_index("dp"), lax.axis_index("mp")
    return mp // NC, dp // NZ, dp % NZ, mp % NC


def device(x, y, z, core):
    return (y * NZ + z, x * NC + core)


def wrap(value, size):
    return lax.rem(value + size, size)


def greet(partners):
    barrier = pltpu.get_barrier_semaphore()
    for partner in partners:
        pl.semaphore_signal(barrier, inc=1, device_id=partner, device_id_type=MESH)
    pl.semaphore_wait(barrier, len(partners))


def remote(src, dst, send_sem, recv_sem, target):
    return pltpu.make_async_remote_copy(
        src_ref=src,
        dst_ref=dst,
        send_sem=send_sem,
        recv_sem=recv_sem,
        device_id=target,
        device_id_type=MESH,
    )


Z_ORDER = (0, 1, 7, 2, 6, 3, 5, 4)


def gather_kernel(
    features, upstream, f_out, u_out, f_y,
    fy_send, fy_recv, fz_send, fz_recv, fx_send, fx_recv,
    uz_send, uz_recv, uy_send, uy_recv, local_sem,
):
    x, y, z, core = place()
    partners = [device(wrap(x + 1, NX), y, z, core), device(wrap(x - 1, NX), y, z, core)]
    partners += [device(x, wrap(y + a, NY), z, core) for a in range(1, NY)]
    partners += [device(x, y, wrap(z + d, NZ), c) for d in range(1, NZ) for c in range(NC)]
    partners += [device(x, y, z, 1 - core)]
    greet(partners)

    sends = []

    def go(copy):
        copy.start()
        sends.append(copy)

    up, down = wrap(y + 1, NY), wrap(y - 1, NY)
    right, left = wrap(x + 1, NX), wrap(x - 1, NX)

    my_tokens = pl.ds(pl.multiple_of(64 * core + 16 * x, 16), 16)

    def f_cols(row):
        return features.at[my_tokens, pl.ds(pl.multiple_of(row * 1024, 1024), 1024)]

    for a in (2, 1, 3):
        row = wrap(y + a, NY)
        go(remote(f_cols(row), f_y.at[y], fy_send.at[a], fy_recv.at[a], device(x, row, z, core)))
    f_own = pltpu.make_async_copy(f_cols(y), f_y.at[y], local_sem.at[0])
    f_own.start()

    parity = wrap(core - z % NC, NC)

    def u_tile(token_half, row):
        column = pl.multiple_of((row // 2) % 2 * BLOCK, BLOCK)
        return upstream.at[pl.ds(64 * token_half, 64), pl.ds(column, BLOCK)]

    here = parity == 0
    for j in (2, 1, 3, 0):
        d = 2 * j + parity
        row = wrap(z + d, NZ)
        for c in range(NC):
            copy = remote(
                u_tile(c, row), u_out.at[y, z], uz_send.at[j, c], uz_recv.at[d], device(x, y, row, c)
            )
            if j == 0:
                mine = here & (core == c)

                @pl.when(mine)
                def _():
                    pltpu.make_async_copy(u_tile(c, z), u_out.at[y, z], local_sem.at[1]).start()

                @pl.when(jnp.logical_not(mine))
                def _():
                    copy.start()
            else:
                go(copy)

    f_own.wait()
    for a in (1, 3, 2):
        origin = wrap(y - a, NY)
        remote(f_cols(y), f_y.at[origin], fy_send.at[a], fy_recv.at[a], device(x, y, z, core)).wait_recv()

    def f_half(row):
        return f_y.at[:, :, pl.ds(pl.multiple_of(row // 4 * BLOCK, BLOCK), BLOCK)]

    for d in (4, 3, 5, 2, 6, 1, 7):
        row = wrap(z + d, NZ)
        go(
            remote(
                f_half(row), f_out.at[:, z, x], fz_send.at[d], fz_recv.at[d], device(x, y, row, core)
            )
        )
    f_keep = pltpu.make_async_copy(f_half(z), f_out.at[:, z, x], local_sem.at[2])
    f_keep.start()

    def u_part(row, origin, part):
        ref = u_out.at[row, origin]
        return ref if part is None else ref.at[pl.ds(32 * part, 32), :]

    def send_u(origin, d, slot, row, part, forward_to):
        ref = u_part(row, origin, part)
        go(remote(ref, ref, uy_send.at[d, slot], uy_recv.at[d, slot], device(x, forward_to, z, core)))

    def wait_u(origin, d, slot, row, part):
        ref = u_part(row, origin, part)
        remote(ref, ref, uy_send.at[d, slot], uy_recv.at[d, slot], device(x, up, z, core)).wait_recv()

    def f_part(column, origin, part):
        return f_out.at[:, origin, column] if part is None else f_out.at[pl.ds(2 * part, 2), origin, column]

    def send_f(origin, d, slot, column, part, forward_to):
        ref = f_part(column, origin, part)
        go(remote(ref, ref, fx_send.at[d, slot], fx_recv.at[d, slot], device(forward_to, y, z, core)))

    def wait_f(origin, d, slot, column, part):
        ref = f_part(column, origin, part)
        remote(ref, ref, fx_send.at[d, slot], fx_recv.at[d, slot], device(right, y, z, core)).wait_recv()

    def u_first(d):
        origin = wrap(z - d, NZ)
        ref = u_out.at[y, origin]
        arrived = remote(ref, ref, uz_send.at[0, 0], uz_recv.at[d], device(x, y, z, core))
        if d == 0:
            mine = z % NC == core

            @pl.when(mine)
            def _():
                pltpu.make_async_copy(ref, ref, local_sem.at[1]).wait()

            @pl.when(jnp.logical_not(mine))
            def _():
                arrived.wait_recv()
        else:
            arrived.wait_recv()
        send_u(origin, d, 0, y, None, up)
        send_u(origin, d, 1, y, None, down)

    def u_second(d):
        origin = wrap(z - d, NZ)
        wait_u(origin, d, 0, down, None)
        send_u(origin, d, 2, down, 0, up)
        wait_u(origin, d, 1, up, None)
        send_u(origin, d, 3, up, 1, down)

    def u_last(d):
        origin = wrap(z - d, NZ)
        far = wrap(y + 2, NY)
        wait_u(origin, d, 2, far, 0)
        wait_u(origin, d, 3, far, 1)

    def f_first(d):
        origin = wrap(z - d, NZ)
        ref = f_out.at[:, origin, x]
        if d == 0:
            f_keep.wait()
        else:
            remote(ref, ref, fz_send.at[d], fz_recv.at[d], device(x, y, z, core)).wait_recv()
        send_f(origin, d, 0, x, None, right)
        send_f(origin, d, 1, x, None, left)

    def f_second(d):
        origin = wrap(z - d, NZ)
        wait_f(origin, d, 0, left, None)
        send_f(origin, d, 2, left, 0, right)
        wait_f(origin, d, 1, right, None)
        send_f(origin, d, 3, right, 1, left)

    def f_last(d):
        origin = wrap(z - d, NZ)
        far = wrap(x + 2, NX)
        wait_f(origin, d, 2, far, 0)
        wait_f(origin, d, 3, far, 1)

    f_first(0)
    for step in range(NZ + 3):
        if step < NZ:
            u_first(Z_ORDER[step])
        if 1 <= step <= NZ - 1:
            f_first(Z_ORDER[step])
        if 1 <= step <= NZ:
            u_second(Z_ORDER[step - 1])
        if 2 <= step <= NZ + 1:
            f_second(Z_ORDER[step - 2])
        if 2 <= step <= NZ + 1:
            u_last(Z_ORDER[step - 2])
        if 3 <= step <= NZ + 2:
            f_last(Z_ORDER[step - 3])

    for copy in sends:
        copy.wait_send()
    for c in range(NC):
        @pl.when(jnp.logical_not(here & (core == c)))
        def _():
            remote(
                u_tile(c, z), u_out.at[y, z], uz_send.at[0, c], uz_recv.at[0], device(x, y, z, 1 - core)
            ).wait_send()


def gather_inputs(features, upstream):
    dma = pltpu.SemaphoreType.DMA
    f_all, u_all = pl.pallas_call(
        gather_kernel,
        out_shape=(
            jax.ShapeDtypeStruct((NY, NZ, NX, 16, BLOCK), jnp.bfloat16),
            jax.ShapeDtypeStruct((NY, NZ, 64, BLOCK), jnp.bfloat16),
        ),
        in_specs=[pl.BlockSpec(memory_space=pl.ANY)] * 2,
        out_specs=(pl.BlockSpec(memory_space=pl.ANY),) * 2,
        scratch_shapes=[
            pltpu.VMEM((NY, 16, 1024), jnp.bfloat16),
            dma((NY,)), dma((NY,)), dma((NZ,)), dma((NZ,)), dma((NZ, 4)), dma((NZ, 4)),
            dma((4, NC)), dma((NZ,)), dma((NZ, 4)), dma((NZ, 4)), dma((3,)),
        ],
        compiler_params=pltpu.CompilerParams(collective_id=0, has_side_effects=True),
    )(features, upstream)
    return f_all.reshape(-1, BLOCK), u_all.reshape(-1, BLOCK)


def spread_plan():
    rows = (ROWS_A, ROWS_B)
    first, second = (0, 1), (1, 0)
    sizes = (NY, NZ)

    def onward(part):
        kind, offsets, half = part
        out = []
        for level, axis in enumerate((first, second)[kind]):
            far = sizes[axis] // 2
            offset = offsets[axis]
            later = (first, second)[kind][level + 1 :]
            if any(offsets[other] != 0 for other in later):
                continue
            for sign in (1, -1):
                if offset * sign > 0 or abs(offset) == far:
                    continue
                moved = list(offsets)
                moved[axis] = offset - sign
                if abs(moved[axis]) == far:
                    moved[axis] = far
                    out.append((axis, sign, (kind, tuple(moved), 0 if sign == 1 else 1)))
                else:
                    out.append((axis, sign, (kind, tuple(moved), None)))
        return out

    return rows, onward


def spread_schedule():
    rows, onward = spread_plan()
    link_free = {}
    events = []
    pending = []
    halves = {}

    def launch(time, part):
        sends = []
        for axis, sign, moved in onward(part):
            count = rows[moved[0]] // (1 if moved[2] is None else 2)
            begin = max(time, link_free.get((axis, sign), 0.0))
            done = begin + count * BLOCK * 2 * 2 / 100e3
            link_free[(axis, sign)] = done
            pending.append((done + 1.0, len(pending), moved))
            sends.append((axis, sign, moved))
        return sends

    start = [launch(0.0, (kind, (0, 0), None)) for kind in (1, 0)]
    while pending:
        pending.sort()
        time, _, part = pending.pop(0)
        kind, offsets, half = part
        if half is not None:
            halves[(kind, offsets)] = halves.get((kind, offsets), 0) + 1
            if halves[(kind, offsets)] == 2:
                events.append((part, launch(time, (kind, offsets, None))))
            else:
                events.append((part, []))
        else:
            events.append((part, launch(time, part)))
    return [send for group in start for send in group], events


def spread_kernel(
    block, sums, out, other_block, shard, mp_sums, y_sums, z_sums, mp_total, y_total,
    mp_send, mp_recv, ys_send, ys_recv, zs_send, zs_recv, swap_sem, send_sem, recv_sem, local_sem,
):
    x, y, z, core = place()
    mp = x * NC + core
    mp_peers = [(y * NZ + z, wrap(mp + j, NX * NC)) for j in range(1, NX * NC)]
    y_peers = [device(x, wrap(y + j, NY), z, core) for j in range(1, NY)]
    z_peers = [device(x, y, wrap(z + j, NZ), core) for j in range(1, NZ)]
    swapped = z % NC != core
    swap_peer = device(x, y, z + 1 - 2 * (z % NC), 1 - core)
    greet(mp_peers + y_peers + z_peers + [swap_peer])

    swap = remote(block, other_block, swap_sem.at[0], swap_sem.at[1], swap_peer)

    @pl.when(swapped)
    def _():
        swap.start()

    def reduce_over(peers, source, slots, sends, recvs):
        copies = [
            remote(source, slots.at[j], sends.at[j], recvs.at[j], peer) for j, peer in enumerate(peers)
        ]
        for copy in copies:
            copy.start()
        total = source[...]
        for j, copy in enumerate(copies):
            copy.wait_recv()
            total = total + slots[j]
        return total, copies

    total, sent_mp = reduce_over(mp_peers, sums, mp_sums, mp_send, mp_recv)
    mp_total[...] = total
    total, sent_y = reduce_over(y_peers, mp_total, y_sums, ys_send, ys_recv)
    y_total[...] = total
    total, sent_z = reduce_over(z_peers, y_total, z_sums, zs_send, zs_recv)
    scale = jnp.sqrt(total[0:1, 0:1] / (total[1:2, 0:1] + 1e-12))

    @pl.when(swapped)
    def _():
        swap.wait()
        shard[...] = (other_block[...] * scale).astype(jnp.bfloat16)

    @pl.when(jnp.logical_not(swapped))
    def _():
        shard[...] = (block[...] * scale).astype(jnp.bfloat16)

    first_row, row_count = (0, ROWS_A), (ROWS_A, ROWS_B)

    def region(part):
        kind, (a, b), half = part
        row, depth = wrap(y + a, NY), wrap(z + b, NZ)
        count = row_count[kind]
        begin = row * 1024 + depth // 4 * BLOCK + depth % 2 * HALF + first_row[kind]
        if half is not None:
            count //= 2
            begin = begin + half * count
        column = pl.multiple_of((depth // 2) % 2 * BLOCK, BLOCK)
        return out.at[pl.ds(pl.multiple_of(begin, 16), count), pl.ds(column, BLOCK)]

    start, events = spread_schedule()
    keys = [part for part, _ in events]
    sent = []

    def send(axis, sign, moved):
        kind, offsets, half = moved
        mine = list(offsets)
        mine[axis] += sign
        if offsets[axis] == (NY, NZ)[axis] // 2:
            mine[axis] = sign * offsets[axis] * -1 + sign
        mine = tuple(mine)
        here = region((kind, mine, half))
        if mine == (0, 0):
            count = row_count[kind] // (1 if half is None else 2)
            source = shard.at[pl.ds(first_row[kind] + (half or 0) * count, count), :]
        else:
            source = here
        target = (
            device(x, wrap(y + sign, NY), z, core) if axis == 0 else device(x, y, wrap(z + sign, NZ), core)
        )
        index = keys.index(moved)
        copy = remote(source, here, send_sem.at[index], recv_sem.at[index], target)
        copy.start()
        sent.append(copy)

    for one in start:
        send(*one)
    whole = pltpu.make_async_copy(
        shard,
        out.at[
            pl.ds(pl.multiple_of(y * 1024 + z // 4 * BLOCK + z % 2 * HALF, HALF), HALF),
            pl.ds(pl.multiple_of((z // 2) % 2 * BLOCK, BLOCK), BLOCK),
        ],
        local_sem.at[0],
    )
    whole.start()
    for index, (part, onward) in enumerate(events):
        here = region(part)
        remote(here, here, send_sem.at[index], recv_sem.at[index], swap_peer).wait_recv()
        for one in onward:
            send(*one)
    for copy in sent + sent_mp + sent_y + sent_z:
        copy.wait_send()
    whole.wait()


def spread_update(block, sums):
    dma = pltpu.SemaphoreType.DMA
    tile = (8, 128)
    count = len(spread_schedule()[1])
    return pl.pallas_call(
        spread_kernel,
        out_shape=jax.ShapeDtypeStruct((NY * NZ * 128, 1024), jnp.bfloat16),
        in_specs=[pl.BlockSpec(memory_space=pltpu.VMEM)] * 2,
        out_specs=pl.BlockSpec(memory_space=pl.ANY),
        scratch_shapes=[
            pltpu.VMEM((HALF, BLOCK), jnp.float32),
            pltpu.VMEM((HALF, BLOCK), jnp.bfloat16),
            pltpu.VMEM((NX * NC, *tile), jnp.float32),
            pltpu.VMEM((NY, *tile), jnp.float32),
            pltpu.VMEM((NZ, *tile), jnp.float32),
            pltpu.VMEM(tile, jnp.float32),
            pltpu.VMEM(tile, jnp.float32),
            dma((NX * NC,)), dma((NX * NC,)), dma((NY,)), dma((NY,)), dma((NZ,)), dma((NZ,)),
            dma((2,)), dma((count,)), dma((count,)), dma((1,)),
        ],
        compiler_params=pltpu.CompilerParams(collective_id=1, has_side_effects=True),
    )(block, sums)


def product(first, second, dims=(1, 0)):
    return lax.dot_general(
        first,
        second,
        (((dims[0],), (dims[1],)), ((), ())),
        precision=lax.Precision.HIGH,
        preferred_element_type=jnp.float32,
    )


def newton_root(stat):
    identity = jnp.eye(stat.shape[-1], dtype=jnp.float32)
    factor = 2.5 / jnp.sqrt(jnp.sum(stat * stat, axis=(-2, -1), keepdims=True))
    iterate = None
    coupled = stat * factor
    for iteration in range(ITERS):
        step_factor = (5.0 * identity - coupled) * 0.25
        iterate = factor**0.25 * step_factor if iterate is None else product(iterate, step_factor)
        if iteration + 1 < ITERS:
            squared = product(step_factor, step_factor)
            coupled = product(squared, product(squared, coupled))
    return iterate


def index_of(y, z, x, core):
    return (y * NZ + z) * NX * NC + x * NC + core


def every():
    return [(y, z, x) for y in range(NY) for z in range(NZ) for x in range(NX)]


BOTH = ("dp", "mp")
SWAP = [
    (index_of(y, z, x, core), index_of(y, z ^ 1, x, 1 - core))
    for y, z, x in every()
    for core in range(NC)
    if z % 2 != core
]
CORES = [
    (index_of(y, z, x, core), index_of(y, z, x, 1 - core)) for y, z, x in every() for core in range(NC)
]


def shards(features, upstream, stats, accum):
    x, y, z, core = place()
    member = z % 4
    swapped = z % NC != core
    left_side = core == 0
    other_stat = lax.ppermute(stats[0, 0], BOTH, SWAP)
    f_all, u_all = gather_inputs(features, upstream)
    over_tokens = functools.partial(
        lax.dot_general,
        dimension_numbers=(((0,), (0,)), ((), ())),
        preferred_element_type=jnp.float32,
    )
    straight, turned = over_tokens(f_all, u_all), over_tokens(u_all, f_all)
    mine = jnp.where(left_side, straight, turned)
    block = mine + lax.ppermute(jnp.where(left_side, turned, straight), BOTH, CORES)

    pieces = []
    for turn in range(4):
        rows = lax.dynamic_slice_in_dim(block, (member + turn) % 4 * 128, 128, 0)
        perm = [
            (index_of(y, z, x, 0), index_of(y, z // 4 * 4 + (z + turn) % 4, x, z % 2)) for y, z, x in every()
        ]
        pieces.append(lax.ppermute(rows, BOTH, perm))
    near, far = pieces[0] + pieces[1], pieces[2] + pieces[3]
    near_first = wrap(member - wrap(member - core, 2), 4) // 2 == 0
    gradient = jnp.concatenate(
        [jnp.where(near_first, near, far), jnp.where(near_first, far, near)], 1
    )
    new_accum = accum + gradient * gradient
    adagrad = gradient / jnp.sqrt(new_accum)

    new_stat = jnp.where(swapped, other_stat, stats[0, 0]) + product(block, block, (1, 1))
    stat_back = lax.ppermute(new_stat, BOTH, SWAP)
    root = newton_root(new_stat)
    other_root = lax.ppermute(root, BOTH, CORES)
    left_root, right_root = jnp.where(left_side, root, other_root), jnp.where(left_side, other_root, root)
    left_rows = lax.dynamic_slice_in_dim(left_root, core * HALF, HALF, 0)
    straight_block = jnp.where(left_side, block, block.T)
    precond = product(product(left_rows, straight_block), right_root)

    totals = jnp.where(
        lax.broadcasted_iota(jnp.int32, (8, 128), 0) == 0, jnp.sum(adagrad * adagrad), jnp.sum(precond * precond)
    )
    update = spread_update(precond, totals)
    return (jnp.where(swapped, stat_back, new_stat)[None, None], new_accum, update)


def solution(mesh):
    placed = (P("dp", None), P("dp", "mp"), P("dp", "mp", None, None), P("dp", "mp"))
    return jax.shard_map(
        shards,
        mesh=mesh,
        in_specs=placed,
        out_specs=(P("dp", "mp", None, None), P("dp", "mp"), P(None, "mp")),
        check_vma=False,
    )
```

time: 665 us -> 215 us (0.32)
  waiting for transfers between devices: 471 us -> 15.3 us
  Pallas kernels: 0 us -> 128 us
  blocking collectives: 77.1 us -> 0 us
  matrix products: 64.4 us -> 34.9 us
  between operations: 16.9 us -> 1.81 us
    reduce_scatter x1 -> x0, waiting for transfers between devices: 247 us -> none  [shards(): lax.psum_scatter(lax.dot_general(features, upstream, (((0,), (0,)), ((),...]
    pallas_call x0 -> x2, Pallas kernels: none -> 128 us  [the longest x1 67.6 us: spread_update(): pl.pallas_call(spread_kernel, out_shape=jax.ShapeDtypeStruct((NY * NZ * 1...]
    ppermute x5 -> x8, waiting for transfers between devices: 132 us -> 15.3 us  [the longest x1 11 us: shards(): other_stat = lax.ppermute(stats[0, 0], BOTH, SWAP)]
    all_gather x1 -> x0, waiting for transfers between devices: 92 us -> none  [shards(): update = lax.all_gather(scaled, 'dp', axis=0, tiled=True)]
    psum x1 -> x0, blocking collectives: 77.1 us -> none  [shards(): lax.psum((jnp.sum(adagrad * adagrad), precond_local), ('dp', 'mp'))]
    dot_general x27 -> x25, matrix products: 64.4 us -> 34.9 us  [the longest x23 29 us: product(): lax.dot_general(first, second, (((dims[0],), (dims[1],)), ((), ())), prec...]
    ppermute x5 -> x8, starting transfers between devices: 11.6 us -> 13.3 us  [the longest x4 8.81 us: shards(): pieces.append(lax.ppermute(rows, BOTH, perm))]
  transfers between devices with their start and end apart: 7 -> 8, of which waited for: 7 -> 3; matrix products, arithmetic and copies ran while one was open for 0% -> 7% of each run, Pallas kernels for 0% -> 32%
where the time goes in v1:
time: 215 us; the launch traced here: 214 us
  Pallas kernels  128 us (60%)
  matrix products  34.9 us (16%)
  waiting for transfers between devices  15.3 us (7%)
  starting transfers between devices  13.3 us (6%)
  local copies, waits for them, and re-layouts  11.6 us (5%)
  other arithmetic  9.08 us (4%)
    pallas_call x1, Pallas kernels, spread_update(): pl.pallas_call(spread_kernel, out_shape=jax.ShapeDtypeStruct((NY * NZ * 1...  67.6 us
    pallas_call x1, Pallas kernels, gather_inputs(): pl.pallas_call(gather_kernel, out_shape=(jax.ShapeDtypeStruct((NY, NZ, NX...  60.7 us
    dot_general x23, matrix products, product(): lax.dot_general(first, second, (((dims[0],), (dims[1],)), ((), ())), prec...  29 us
    ppermute x1, waiting for transfers between devices, shards(): other_stat = lax.ppermute(stats[0, 0], BOTH, SWAP)  11 us
    ppermute x4, starting transfers between devices, shards(): pieces.append(lax.ppermute(rows, BOTH, perm))  8.81 us
    unnamed x9, local copies, waits for them, and re-layouts  8.74 us
    dot_general x2, matrix products, shards(): straight, turned = (over_tokens(f_all, u_all), over_tokens(u_all, f_all))  5.89 us
  transfers between devices with their start and end apart: 8, of which 3 were waited for; matrix products, arithmetic and copies ran while one was open for 7% of the time, Pallas kernels for 32%

profile of v1, /device:TPU:32, one launch (start us, length us, event | category | flops | bytes accessed | tf_op | source)
XLA Modules:
  0.0 214.3 jit_solution(6280950380882180284)
XLA Ops:
  0.6 60.7 %shard_map.67 = (bf16[4,8,4,16,512]{4,3,2,1,0:T(8,128)(2,1)}, bf16[4,8,64,512]{3,2,1,0:T(8,128)(2,1)}) custom-call(bf16[128,4096]{1,0:T(8,128)(2,1)} %features.1, bf16[128,1024]{1,0:T(8,128)(2,1)} %upstream.1), custom_call_target="tpu_custom_call" | custom-call | tf_op jit(solution)/shard_map/pallas_call | solution.py:235
  61.4 0.0 copy-start.1
  61.4 0.0 copy-start.2
  61.4 3.6 %fusion.92 = f32[512,512]{1,0:T(8,128)S(1)} fusion(bf16[2048,512]{1,0:T(8,128)(2,1)} %bitcast.41, bf16[2048,512]{1,0:T(8,128)(2,1)} %bitcast.43), kind=kOutput, calls=%fused_computation.109 | convolution fusion | flops 1073741824 | bytes 5242880 | tf_op jit(solution)/shard_map/dot_general | solution.py:502
  65.0 0.0 copy-done.1
  65.0 0.0 copy-done.2
  65.1 2.2 %broadcast_select_fusion = (f32[512,512]{1,0:T(8,128)}, f32[512,512]{1,0:T(8,128)S(1)}) fusion(f32[512,512]{1,0:T(8,128)S(1)} %fusion.92, pred[]{:T(512)S(6)} %eq.35, bf16[2048,512]{1,0:T(8,128)(2,1)S(1)} %bitcast.44, bf16[2048,512]{1,0:T(8,128)(2,1)S(1)} %bitcast.42), kind=kOutput, calls=%fused_computation.72 | convolution fusion | flops 1074003968 | bytes 7340033 | tf_op jit(solution)/shard_map/dot_general | solution.py:502
  67.3 0.0 collective-permute-start.1
  67.3 2.1 collective-permute-start
  69.4 0.7 collective-permute-done.1
  70.2 0.0 copy-start.3
  70.2 1.0 copy-done.3
  71.1 1.6 select_add_fusion
  72.7 11.0 %collective-permute-done = f32[512,512]{1,0:T(8,128)} collective-permute-done((f32[512,512]{1,0:T(8,128)}, f32[512,512]{1,0:T(8,128)}, u32[]{:S(2)}, u32[]{:S(2)}) %collective-permute-start) | collective-permute-done | bytes 1048608 | tf_op jit(solution)/shard_map/ppermute | solution.py:495
  83.7 3.3 %multiply_reduce_fusion = (f32[]{:T(128)}, f32[512,512]{1,0:T(8,128)S(1)}) fusion(f32[512,512]{1,0:T(8,128)} %collective-permute-done, f32[1,1,512,512]{3,2,1,0:T(8,128)} %param.6, pred[]{:T(512)S(6)} %ne.48, f32[512,512]{1,0:T(8,128)S(1)} %select_add_fusion), kind=kOutput, calls=%fused_computation.19 | convolution fusion | flops 806354944 | bytes 4194309 | tf_op jit(solution)/shard_map/dot_general | solution.py:447
  87.8 1.1 fusion.8
  88.9 1.0 fusion.12
  89.9 1.0 fusion.93
  90.9 1.0 fusion.26
  92.0 1.1 fusion.10
  93.1 1.0 fusion.94
  94.1 1.0 fusion.95
  95.1 1.0 fusion.22
  96.1 1.0 fusion.24
  97.2 1.0 fusion.96
  98.2 1.2 fusion.97
  99.4 1.0 fusion.18
  100.5 1.0 fusion.20
  101.5 1.0 fusion.98
  102.6 1.0 fusion.99
  103.6 1.0 fusion.14
  104.6 1.0 fusion.16
  105.7 1.0 fusion.100
  106.7 1.0 fusion
  107.7 1.0 fusion.101
  108.7 0.1 collective-permute-start.7
  108.9 0.9 constant_dynamic-slice_fusion.2
  109.8 2.9 %collective-permute-start.4 = (f32[128,512]{1,0:T(8,128)}, f32[128,512]{1,0:T(8,128)}, u32[]{:S(2)}, u32[]{:S(2)}) collective-permute-start(f32[128,512]{1,0:T(8,128)} %get-tuple-element.13), channel_id=1, source_target_pairs={{0,8},{2,10},{4,12},{6,14},{8,17},{10,19},{12,21},{14,23},{16,24},... | collective-permute-start | bytes 786440 | tf_op jit(solution)/shard_map/ppermute | solution.py:512
  112.7 1.9 collective-permute-start.6
  114.6 2.0 collective-permute-start.5
  116.7 2.0 collective-permute-start.3
  118.7 1.3 copy.7
  120.0 0.0 copy-start
  120.0 0.0 collective-permute-done.4
  120.0 2.3 %collective-permute-start.2 = (f32[512,512]{1,0:T(8,128)S(1)}, f32[512,512]{1,0:T(8,128)}, u32[]{:S(2)}, u32[]{:S(2)}) collective-permute-start(f32[512,512]{1,0:T(8,128)S(1)} %get-tuple-element.10), channel_id=1, source_target_pairs={{1,8},{3,10},{5,12},{7,14},{8,1},{10,3},{12,5},{14,7},{17,24},{19,... | collective-permute-start | bytes 3145736 | tf_op jit(solution)/shard_map/ppermute | solution.py:522
  122.3 0.0 collective-permute-done.6
  122.3 3.5 %collective-permute-done.5 = f32[128,512]{1,0:T(8,128)} collective-permute-done((f32[128,512]{1,0:T(8,128)}, f32[128,512]{1,0:T(8,128)}, u32[]{:S(2)}, u32[]{:S(2)}) %collective-permute-start.5) | collective-permute-done | bytes 262176 | tf_op jit(solution)/shard_map/ppermute | solution.py:512
  125.8 0.0 collective-permute-done.3
  125.8 1.3 broadcast_select_fusion.2
  127.1 2.5 %multiply_reduce_fusion.2 = (f32[]{:T(128)}, f32[128,1024]{1,0:T(8,128)}) fusion(f32[128,512]{1,0:T(8,128)S(1)} %get-tuple-element.12, f32[128,512]{1,0:T(8,128)S(1)} %get-tuple-element.11, f32[128,1024]{1,0:T(8,128)} %param.7), kind=kLoop, calls=%fused_computation.37 | loop fusion | flops 786431 | bytes 1572868 | tf_op jit(solution)/shard_map/reduce_sum | solution.py:531
  129.6 0.0 collective-permute-done.7
  129.6 0.0 copy-done
  129.6 1.7 fusion.5
  131.3 3.3 %multiply_reduce_fusion.1 = (f32[]{:T(128)}, f32[256,512]{1,0:T(8,128)}) fusion(f32[256,512]{1,0:T(8,128)S(1)} %fusion.5, f32[512,512]{1,0:T(8,128)} %collective-permute-done.7, f32[512,512]{1,0:T(8,128)S(1)} %fusion.101, pred[]{:T(512)S(6)} %eq.35), kind=kOutput, calls=%fused_computation.36 | convolution fusion | flops 403177472 | bytes 3145733 | tf_op jit(solution)/shard_map/dot_general | solution.py:447
  134.6 1.3 compare_select_fusion
  135.9 0.7 iota.39.sums
  136.5 67.6 %shard_map.68 = bf16[4096,1024]{1,0:T(8,128)(2,1)} custom-call(f32[256,512]{1,0:T(8,128)} %get-tuple-element.20.block, f32[8,128]{1,0:T(8,128)} %iota.39.sums), custom_call_target="tpu_custom_call" | custom-call | tf_op jit(solution)/shard_map/pallas_call | solution.py:426
  204.1 0.0 collective-permute-done.2
  204.1 2.4 %select_bitcast_fusion = f32[1,1,512,512]{3,2,1,0:T(8,128)} fusion(f32[512,512]{1,0:T(8,128)} %collective-permute-done.2, f32[512,512]{1,0:T(8,128)S(1)} %get-tuple-element.10, pred[]{:T(512)S(6)} %ne.48), kind=kLoop, calls=%fused_computation.21 | loop fusion | flops 262144 | bytes 3145729 | tf_op jit(solution)/shard_map/broadcast_in_dim | solution.py:534
  206.6 7.8 %copy.9 = bf16[4096,1024]{1,0:T(8,128)(2,1)} copy(bf16[4096,1024]{1,0:T(8,128)(2,1)} %shard_map.68) | data formatting | bytes 16777216
Async XLA Ops:
  61.4 3.7 %copy-start.1 = (bf16[4,8,4,16,512]{4,3,2,1,0:T(8,128)(2,1)S(1)}, bf16[4,8,4,16,512]{4,3,2,1,0:T(8,128)(2,1)}, u32[]{:S(2)}) copy-start(bf16[4,8,4,16,512]{4,3,2,1,0:T(8,128)(2,1)} %get-tuple-element.5) | copy-start | bytes 6291460
  61.4 3.7 %copy-start.2 = (bf16[4,8,64,512]{3,2,1,0:T(8,128)(2,1)S(1)}, bf16[4,8,64,512]{3,2,1,0:T(8,128)(2,1)}, u32[]{:S(2)}) copy-start(bf16[4,8,64,512]{3,2,1,0:T(8,128)(2,1)} %get-tuple-element.6) | copy-start | bytes 6291460
  67.3 2.9 %collective-permute-start.1 = (f32[512,512]{1,0:T(8,128)}, f32[512,512]{1,0:T(8,128)S(1)}, u32[]{:S(2)}, u32[]{:S(2)}) collective-permute-start(f32[512,512]{1,0:T(8,128)} %get-tuple-element.17), channel_id=1, source_target_pairs={{0,1},{1,0},{2,3},{3,2},{4,5},{5,4},{6,7},{7,6},{8,9},{9,8},{10,11... | collective-permute-start | bytes 3145736 | tf_op jit(solution)/shard_map/ppermute | solution.py:504
  67.3 16.4 %collective-permute-start = (f32[512,512]{1,0:T(8,128)}, f32[512,512]{1,0:T(8,128)}, u32[]{:S(2)}, u32[]{:S(2)}) collective-permute-start(f32[512,512]{1,0:T(8,128)} %bitcast), channel_id=1, source_target_pairs={{1,8},{3,10},{5,12},{7,14},{8,1},{10,3},{12,5},{14,7},{17,24},{19,... | collective-permute-start | bytes 3145736 | tf_op jit(solution)/shard_map/ppermute | solution.py:495
  70.2 1.0 copy-start.3
  108.7 20.9 %collective-permute-start.7 = (f32[512,512]{1,0:T(8,128)S(1)}, f32[512,512]{1,0:T(8,128)}, u32[]{:S(2)}, u32[]{:S(2)}) collective-permute-start(f32[512,512]{1,0:T(8,128)S(1)} %fusion.101), channel_id=1, source_target_pairs={{0,1},{1,0},{2,3},{3,2},{4,5},{5,4},{6,7},{7,6},{8,9},{9,8},{10,11... | collective-permute-start | bytes 3145736 | tf_op jit(solution)/shard_map/ppermute | solution.py:524
  109.8 10.1 %collective-permute-start.4 = (f32[128,512]{1,0:T(8,128)}, f32[128,512]{1,0:T(8,128)}, u32[]{:S(2)}, u32[]{:S(2)}) collective-permute-start(f32[128,512]{1,0:T(8,128)} %get-tuple-element.13), channel_id=1, source_target_pairs={{0,8},{2,10},{4,12},{6,14},{8,17},{10,19},{12,21},{14,23},{16,24},... | collective-permute-start | bytes 786440 | tf_op jit(solution)/shard_map/ppermute | solution.py:512
  112.7 9.6 %collective-permute-start.6 = (f32[128,512]{1,0:T(8,128)}, f32[128,512]{1,0:T(8,128)}, u32[]{:S(2)}, u32[]{:S(2)}) collective-permute-start(f32[128,512]{1,0:T(8,128)} %get-tuple-element.14), channel_id=1, source_target_pairs={{0,24},{2,26},{4,28},{6,30},{8,1},{10,3},{12,5},{14,7},{16,8},{18,... | collective-permute-start | bytes 786440 | tf_op jit(solution)/shard_map/ppermute | solution.py:512
  114.6 11.2 %collective-permute-start.5 = (f32[128,512]{1,0:T(8,128)}, f32[128,512]{1,0:T(8,128)}, u32[]{:S(2)}, u32[]{:S(2)}) collective-permute-start(f32[128,512]{1,0:T(8,128)} %get-tuple-element.15), channel_id=1, source_target_pairs={{0,16},{2,18},{4,20},{6,22},{8,25},{10,27},{12,29},{14,31},{16,0},... | collective-permute-start | bytes 786440 | tf_op jit(solution)/shard_map/ppermute | solution.py:512
  116.7 9.1 %collective-permute-start.3 = (f32[128,512]{1,0:T(8,128)S(1)}, f32[128,512]{1,0:T(8,128)}, u32[]{:S(2)}, u32[]{:S(2)}) collective-permute-start(f32[128,512]{1,0:T(8,128)S(1)} %get-tuple-element.16), channel_id=1, source_target_pairs={{0,0},{2,2},{4,4},{6,6},{8,9},{10,11},{12,13},{14,15},{16,16},{18,... | collective-permute-start | bytes 786440 | tf_op jit(solution)/shard_map/ppermute | solution.py:512
  120.0 9.7 %copy-start = (f32[512,512]{0,1:T(8,128)S(1)}, f32[512,512]{0,1:T(8,128)}, u32[]{:S(2)}) copy-start(f32[512,512]{0,1:T(8,128)} %copy.7) | copy-start | bytes 3145732
  120.0 84.2 %collective-permute-start.2 = (f32[512,512]{1,0:T(8,128)S(1)}, f32[512,512]{1,0:T(8,128)}, u32[]{:S(2)}, u32[]{:S(2)}) collective-permute-start(f32[512,512]{1,0:T(8,128)S(1)} %get-tuple-element.10), channel_id=1, source_target_pairs={{1,8},{3,10},{5,12},{7,14},{8,1},{10,3},{12,5},{14,7},{17,24},{19,... | collective-permute-start | bytes 3145736 | tf_op jit(solution)/shard_map/ppermute | solution.py:522

commit v2 on v1

--- a/solution.py
+++ b/solution.py
@@ -51,7 +51,7 @@
 
 
 def gather_kernel(
-    features, upstream, f_out, u_out, f_y,
+    features, upstream, stats, f_out, u_out, stat_out, f_y, stat_send, stat_recv,
     fy_send, fy_recv, fz_send, fz_recv, fx_send, fx_recv,
     uz_send, uz_recv, uy_send, uy_recv, local_sem,
 ):
@@ -70,6 +70,23 @@
 
     up, down = wrap(y + 1, NY), wrap(y - 1, NY)
     right, left = wrap(x + 1, NX), wrap(x - 1, NX)
+
+    swapped = z % NC != core
+
+    def stat_rows(i):
+        return pl.ds(128 * i, 128), pl.ds(128 * i, BLOCK - 128 * i)
+
+    stat_copies = [
+        remote(
+            stats.at[stat_rows(i)],
+            stat_out.at[stat_rows(i)],
+            stat_send.at[i],
+            stat_recv.at[i],
+            device(x, y, z + 1 - 2 * (z % NC), 1 - core),
+        )
+        for i in range(4)
+    ]
+    stat_keep = pltpu.make_async_copy(stats, stat_out, local_sem.at[3])
 
     my_tokens = pl.ds(pl.multiple_of(64 * core + 16 * x, 16), 16)
 
@@ -108,6 +125,15 @@
                     copy.start()
             else:
                 go(copy)
+
+    @pl.when(swapped)
+    def _():
+        for copy in stat_copies:
+            copy.start()
+
+    @pl.when(jnp.logical_not(swapped))
+    def _():
+        stat_keep.start()
 
     f_own.wait()
     for a in (1, 3, 2):
@@ -220,6 +246,15 @@
         if 3 <= step <= NZ + 2:
             f_last(Z_ORDER[step - 3])
 
+    @pl.when(swapped)
+    def _():
+        for copy in stat_copies:
+            copy.wait()
+
+    @pl.when(jnp.logical_not(swapped))
+    def _():
+        stat_keep.wait()
+
     for copy in sends:
         copy.wait_send()
     for c in range(NC):
@@ -230,24 +265,26 @@
             ).wait_send()
 
 
-def gather_inputs(features, upstream):
+def gather_inputs(features, upstream, stats):
     dma = pltpu.SemaphoreType.DMA
-    f_all, u_all = pl.pallas_call(
+    f_all, u_all, stat = pl.pallas_call(
         gather_kernel,
         out_shape=(
             jax.ShapeDtypeStruct((NY, NZ, NX, 16, BLOCK), jnp.bfloat16),
             jax.ShapeDtypeStruct((NY, NZ, 64, BLOCK), jnp.bfloat16),
+            jax.ShapeDtypeStruct((BLOCK, BLOCK), jnp.float32),
         ),
-        in_specs=[pl.BlockSpec(memory_space=pl.ANY)] * 2,
-        out_specs=(pl.BlockSpec(memory_space=pl.ANY),) * 2,
+        in_specs=[pl.BlockSpec(memory_space=pl.ANY)] * 3,
+        out_specs=(pl.BlockSpec(memory_space=pl.ANY),) * 3,
         scratch_shapes=[
             pltpu.VMEM((NY, 16, 1024), jnp.bfloat16),
+            dma((4,)), dma((4,)),
             dma((NY,)), dma((NY,)), dma((NZ,)), dma((NZ,)), dma((NZ, 4)), dma((NZ, 4)),
-            dma((4, NC)), dma((NZ,)), dma((NZ, 4)), dma((NZ, 4)), dma((3,)),
+            dma((4, NC)), dma((NZ,)), dma((NZ, 4)), dma((NZ, 4)), dma((4,)),
         ],
         compiler_params=pltpu.CompilerParams(collective_id=0, has_side_effects=True),
-    )(features, upstream)
-    return f_all.reshape(-1, BLOCK), u_all.reshape(-1, BLOCK)
+    )(features, upstream, stats)
+    return f_all.reshape(-1, BLOCK), u_all.reshape(-1, BLOCK), stat
 
 
 def spread_plan():
@@ -313,8 +350,47 @@
     return [send for group in start for send in group], events
 
 
-def spread_kernel(
-    block, sums, out, other_block, shard, mp_sums, y_sums, z_sums, mp_total, y_total,
+def split(value):
+    high = value.astype(jnp.bfloat16)
+    return high, (value - high.astype(jnp.float32)).astype(jnp.bfloat16)
+
+
+def product(first, second):
+    dot = functools.partial(jnp.dot, preferred_element_type=jnp.float32)
+    return dot(first[0], second[0]) + (dot(first[0], second[1]) + dot(first[1], second[0]))
+
+
+def newton_root(stat, iterate, coupled):
+    def advance(now, now_parts):
+        change = split((product(now_parts, now_parts) - 10.0 * now) * (1 / 16))
+        once = (25 / 16) * now + product(change, now_parts)
+        return (25 / 16) * once + product(change, split(once))
+
+    start = stat[...]
+    factor = 2.5 / jnp.sqrt(jnp.sum(start * start, keepdims=True))
+    start = start * factor
+    shape = (BLOCK, BLOCK)
+    diagonal = lax.broadcasted_iota(jnp.int32, shape, 0) == lax.broadcasted_iota(jnp.int32, shape, 1)
+    iterate[...] = jnp.sqrt(jnp.sqrt(factor)) * (jnp.where(diagonal, 1.25, 0.0) - 0.25 * start)
+    coupled[...] = advance(start, split(start))
+
+    def body(_, carry):
+        now, root = coupled[...], iterate[...]
+        now_parts = split(now)
+        iterate[...] = 1.25 * root - 0.25 * product(split(root), now_parts)
+        coupled[...] = advance(now, now_parts)
+        return carry
+
+    lax.fori_loop(0, ITERS - 2, body, 0)
+    root = iterate[...]
+    iterate[...] = 1.25 * root - 0.25 * product(split(root), split(coupled[...]))
+
+
+def step_kernel(
+    partial, stats, accum, out, new_stat, new_accum,
+    partial_other, block, stat, iterate, coupled, root_other, pieces, precond, sums,
+    other_block, shard, mp_sums, y_sums, z_sums, mp_total, y_total,
+    core_sem, piece_send, piece_recv, stat_sem, root_sem,
     mp_send, mp_recv, ys_send, ys_recv, zs_send, zs_recv, swap_sem, send_sem, recv_sem, local_sem,
 ):
     x, y, z, core = place()
@@ -323,10 +399,115 @@
     y_peers = [device(x, wrap(y + j, NY), z, core) for j in range(1, NY)]
     z_peers = [device(x, y, wrap(z + j, NZ), core) for j in range(1, NZ)]
     swapped = z % NC != core
+    straight = jnp.logical_not(swapped)
+    left_side = core == 0
+    right_side = core == 1
+    other_core = device(x, y, z, 1 - core)
     swap_peer = device(x, y, z + 1 - 2 * (z % NC), 1 - core)
     greet(mp_peers + y_peers + z_peers + [swap_peer])
 
-    swap = remote(block, other_block, swap_sem.at[0], swap_sem.at[1], swap_peer)
+    exchange = remote(partial, partial_other, core_sem.at[0], core_sem.at[1], other_core)
+    exchange.start()
+    shape = (BLOCK, BLOCK)
+    below = lax.broadcasted_iota(jnp.int32, shape, 0) // 128 > lax.broadcasted_iota(jnp.int32, shape, 1) // 128
+    kept = stats[...]
+    stat[...] = jnp.where(below & swapped, kept.T, kept)
+    exchange.wait()
+    both = partial[...] + partial_other[...]
+    block[...] = both
+
+    member, quad, column = z % 4, z // 4 * 4, (z // 2) % 2
+
+    def piece_rows(row):
+        return block.at[pl.ds(pl.multiple_of(row * 128, 128), 128), :]
+
+    piece_copies = []
+    for j in range(1, 4):
+        row = wrap(member + j, 4)
+        piece_copies.append(
+            remote(
+                piece_rows(row), pieces.at[column], piece_send.at[j], piece_recv.at[column],
+                device(x, y, quad + row, core),
+            )
+        )
+    piece_keep = pltpu.make_async_copy(piece_rows(member), pieces.at[column], piece_send.at[0])
+
+    @pl.when(straight)
+    def _():
+        for copy in piece_copies:
+            copy.start()
+        piece_keep.start()
+
+    turned = both.T
+    first = jnp.where(left_side, both, turned)
+    second = jnp.where(left_side, turned, both)
+    stat[...] = stat[...] + product(split(first), split(second))
+    stat_back = remote(stat, new_stat, stat_sem.at[0], stat_sem.at[1], swap_peer)
+
+    @pl.when(swapped)
+    def _():
+        stat_back.start()
+
+    @pl.when(straight)
+    def _():
+        new_stat[...] = stat[...]
+
+    newton_root(stat, iterate, coupled)
+
+    lower = pl.ds(HALF, HALF)
+    upper = pl.ds(0, HALF)
+    left_sent = remote(
+        iterate.at[lower, :], root_other.at[upper, :], root_sem.at[0], root_sem.at[1], other_core
+    )
+    right_sent = remote(iterate, root_other, root_sem.at[0], root_sem.at[1], other_core)
+
+    @pl.when(left_side)
+    def _():
+        left_sent.start()
+
+    @pl.when(right_side)
+    def _():
+        right_sent.start()
+
+    for c in range(2):
+        origin = 2 * c + core
+
+        @pl.when(origin == member)
+        def _():
+            piece_keep.wait()
+
+        @pl.when(origin != member)
+        def _():
+            remote(pieces.at[c], pieces.at[c], piece_send.at[1], piece_recv.at[c], other_core).wait_recv()
+
+    adagrad_total = jnp.zeros((1, 1), jnp.float32)
+    for c in range(2):
+        columns = slice(c * BLOCK, (c + 1) * BLOCK)
+        squares = pieces[c] * pieces[c]
+        grown = accum[:, columns] + squares
+        new_accum[:, columns] = grown
+        adagrad_total = adagrad_total + jnp.sum(squares / grown, keepdims=True)
+
+    @pl.when(left_side)
+    def _():
+        rows = product(split(iterate[upper, :]), split(block[...]))
+        left_sent.wait_send()
+        right_sent.wait_recv()
+        precond[...] = product(split(rows), split(root_other[...]))
+
+    @pl.when(right_side)
+    def _():
+        columns = product(split(block[...]), split(iterate[...]))
+        right_sent.wait_send()
+        left_sent.wait_recv()
+        precond[...] = product(split(root_other[upper, :]), split(columns))
+
+    precond_total = jnp.sum(precond[...] * precond[...], keepdims=True)
+    sums[...] = jnp.where(
+        lax.broadcasted_iota(jnp.int32, sums.shape, 0) == 0, adagrad_total, precond_total
+    )
+
+    swap = remote(precond, other_block, swap_sem.at[0], swap_sem.at[1], swap_peer)
 
     @pl.when(swapped)
     def _():
@@ -356,9 +537,9 @@
         swap.wait()
         shard[...] = (other_block[...] * scale).astype(jnp.bfloat16)
 
-    @pl.when(jnp.logical_not(swapped))
-    def _():
-        shard[...] = (block[...] * scale).astype(jnp.bfloat16)
+    @pl.when(straight)
+    def _():
+        shard[...] = (precond[...] * scale).astype(jnp.bfloat16)
 
     first_row, row_count = (0, ROWS_A), (ROWS_A, ROWS_B)
 
@@ -418,17 +599,36 @@
         copy.wait_send()
     whole.wait()
 
-
-def spread_update(block, sums):
+    @pl.when(swapped)
+    def _():
+        stat_back.wait()
+
+    @pl.when(straight)
+    def _():
+        for copy in piece_copies:
+            copy.wait_send()
+
+
+def take_step(partial, stats, accum):
     dma = pltpu.SemaphoreType.DMA
     tile = (8, 128)
     count = len(spread_schedule()[1])
+    square = pltpu.VMEM((BLOCK, BLOCK), jnp.float32)
+    vmem = pl.BlockSpec(memory_space=pltpu.VMEM)
     return pl.pallas_call(
-        spread_kernel,
-        out_shape=jax.ShapeDtypeStruct((NY * NZ * 128, 1024), jnp.bfloat16),
-        in_specs=[pl.BlockSpec(memory_space=pltpu.VMEM)] * 2,
-        out_specs=pl.BlockSpec(memory_space=pl.ANY),
+        step_kernel,
+        out_shape=(
+            jax.ShapeDtypeStruct((NY * NZ * 128, 1024), jnp.bfloat16),
+            jax.ShapeDtypeStruct((BLOCK, BLOCK), jnp.float32),
+            jax.ShapeDtypeStruct(accum.shape, jnp.float32),
+        ),
+        in_specs=[vmem] * 3,
+        out_specs=(pl.BlockSpec(memory_space=pl.ANY), vmem, vmem),
         scratch_shapes=[
+            square, square, square, square, square, square,
+            pltpu.VMEM((2, 128, BLOCK), jnp.float32),
+            pltpu.VMEM((HALF, BLOCK), jnp.float32),
+            pltpu.VMEM(tile, jnp.float32),
             pltpu.VMEM((HALF, BLOCK), jnp.float32),
             pltpu.VMEM((HALF, BLOCK), jnp.bfloat16),
             pltpu.VMEM((NX * NC, *tile), jnp.float32),
@@ -436,102 +636,23 @@
             pltpu.VMEM((NZ, *tile), jnp.float32),
             pltpu.VMEM(tile, jnp.float32),
             pltpu.VMEM(tile, jnp.float32),
+            dma((2,)), dma((4,)), dma((2,)), dma((2,)), dma((2,)),
             dma((NX * NC,)), dma((NX * NC,)), dma((NY,)), dma((NY,)), dma((NZ,)), dma((NZ,)),
             dma((2,)), dma((count,)), dma((count,)), dma((1,)),
         ],
-        compiler_params=pltpu.CompilerParams(collective_id=1, has_side_effects=True),
-    )(block, sums)
-
-
-def product(first, second, dims=(1, 0)):
-    return lax.dot_general(
-        first,
-        second,
-        (((dims[0],), (dims[1],)), ((), ())),
-        precision=lax.Precision.HIGH,
-        preferred_element_type=jnp.float32,
+        compiler_params=pltpu.CompilerParams(
+            collective_id=1, has_side_effects=True, vmem_limit_bytes=48 * 2**20
+        ),
+    )(partial, stats, accum)
+
+
+def shards(features, upstream, stats, accum):
+    f_all, u_all, stat = gather_inputs(features, upstream, stats[0, 0])
+    partial = lax.dot_general(
+        f_all, u_all, (((0,), (0,)), ((), ())), preferred_element_type=jnp.float32
     )
-
-
-def newton_root(stat):
-    identity = jnp.eye(stat.shape[-1], dtype=jnp.float32)
-    factor = 2.5 / jnp.sqrt(jnp.sum(stat * stat, axis=(-2, -1), keepdims=True))
-    iterate = None
-    coupled = stat * factor
-    for iteration in range(ITERS):
-        step_factor = (5.0 * identity - coupled) * 0.25
-        iterate = factor**0.25 * step_factor if iterate is None else product(iterate, step_factor)
-        if iteration + 1 < ITERS:
-            squared = product(step_factor, step_factor)
-            coupled = product(squared, product(squared, coupled))
-    return iterate
-
-
-def index_of(y, z, x, core):
-    return (y * NZ + z) * NX * NC + x * NC + core
-
-
-def every():
-    return [(y, z, x) for y in range(NY) for z in range(NZ) for x in range(NX)]
-
-
-BOTH = ("dp", "mp")
-SWAP = [
-    (index_of(y, z, x, core), index_of(y, z ^ 1, x, 1 - core))
-    for y, z, x in every()
-    for core in range(NC)
-    if z % 2 != core
-]
-CORES = [
-    (index_of(y, z, x, core), index_of(y, z, x, 1 - core)) for y, z, x in every() for core in range(NC)
-]
-
-
-def shards(features, upstream, stats, accum):
-    x, y, z, core = place()
-    member = z % 4
-    swapped = z % NC != core
-    left_side = core == 0
-    other_stat = lax.ppermute(stats[0, 0], BOTH, SWAP)
-    f_all, u_all = gather_inputs(features, upstream)
-    over_tokens = functools.partial(
-        lax.dot_general,
-        dimension_numbers=(((0,), (0,)), ((), ())),
-        preferred_element_type=jnp.float32,
-    )
-    straight, turned = over_tokens(f_all, u_all), over_tokens(u_all, f_all)
-    mine = jnp.where(left_side, straight, turned)
-    block = mine + lax.ppermute(jnp.where(left_side, turned, straight), BOTH, CORES)
-
-    pieces = []
-    for turn in range(4):
-        rows = lax.dynamic_slice_in_dim(block, (member + turn) % 4 * 128, 128, 0)
-        perm = [
-            (index_of(y, z, x, 0), index_of(y, z // 4 * 4 + (z + turn) % 4, x, z % 2)) for y, z, x in every()
-        ]
-        pieces.append(lax.ppermute(rows, BOTH, perm))
-    near, far = pieces[0] + pieces[1], pieces[2] + pieces[3]
-    near_first = wrap(member - wrap(member - core, 2), 4) // 2 == 0
-    gradient = jnp.concatenate(
-        [jnp.where(near_first, near, far), jnp.where(near_first, far, near)], 1
-    )
-    new_accum = accum + gradient * gradient
-    adagrad = gradient / jnp.sqrt(new_accum)
-
-    new_stat = jnp.where(swapped, other_stat, stats[0, 0]) + product(block, block, (1, 1))
-    stat_back = lax.ppermute(new_stat, BOTH, SWAP)
-    root = newton_root(new_stat)
-    other_root = lax.ppermute(root, BOTH, CORES)
-    left_root, right_root = jnp.where(left_side, root, other_root), jnp.where(left_side, other_root, root)
-    left_rows = lax.dynamic_slice_in_dim(left_root, core * HALF, HALF, 0)
-    straight_block = jnp.where(left_side, block, block.T)
-    precond = product(product(left_rows, straight_block), right_root)
-
-    totals = jnp.where(
-        lax.broadcasted_iota(jnp.int32, (8, 128), 0) == 0, jnp.sum(adagrad * adagrad), jnp.sum(precond * precond)
-    )
-    update = spread_update(precond, totals)
-    return (jnp.where(swapped, stat_back, new_stat)[None, None], new_accum, update)
+    update, new_stat, new_accum = take_step(partial, stat, accum)
+    return (new_stat[None, None], new_accum, update)
 
 
 def solution(mesh):

time: 215 us -> 169 us (0.79)
  matrix products: 34.9 us -> 3.61 us
  Pallas kernels: 128 us -> 155 us
  waiting for transfers between devices: 15.3 us -> 0 us
  starting transfers between devices: 13.3 us -> 0 us
  other arithmetic: 9.08 us -> 0 us
    dot_general x25 -> x1, matrix products: 34.9 us -> 3.61 us  [shards(): lax.dot_general(f_all, u_all, (((0,), (0,)), ((), ())), preferred_element...]
    pallas_call x1, Pallas kernels: 67.6 us -> 93.8 us  [take_step(): pl.pallas_call(step_kernel, out_shape=(jax.ShapeDtypeStruct((NY * NZ * 12...]
    ppermute x8 -> x0, waiting for transfers between devices: 15.3 us -> none  [the longest x1 11 us: shards(): other_stat = lax.ppermute(stats[0, 0], BOTH, SWAP)]
    ppermute x8 -> x0, starting transfers between devices: 13.3 us -> none  [the longest x4 8.81 us: shards(): pieces.append(lax.ppermute(rows, BOTH, perm))]
    select_n x2 -> x0, other arithmetic: 2.56 us -> none  [the longest x1 1.28 us: shards(): jnp.where(lax.broadcasted_iota(jnp.int32, (8, 128), 0) == 0, jnp.sum(adag...]
    reduce_sum x1 -> x0, other arithmetic: 2.53 us -> none  [shards(): jnp.sum(adagrad * adagrad)]
    broadcast_in_dim x1 -> x0, other arithmetic: 2.41 us -> none  [shards(): jnp.where(swapped, stat_back, new_stat)[None, None]]
    unnamed x9 -> x7, local copies, waits for them, and re-layouts: 8.74 us -> 9.53 us
  transfers between devices with their start and end apart: 8 -> 0, of which waited for: 3 -> 0; matrix products, arithmetic and copies ran while one was open for 7% -> 0% of each run, Pallas kernels for 32% -> 0%
where the time goes in v2:
time: 169 us
  Pallas kernels  155 us (92%)
  local copies, waits for them, and re-layouts  9.53 us (6%)
  matrix products  3.61 us (2%)
    pallas_call x1, Pallas kernels, take_step(): pl.pallas_call(step_kernel, out_shape=(jax.ShapeDtypeStruct((NY * NZ * 12...  93.8 us
    pallas_call x1, Pallas kernels, gather_inputs(): pl.pallas_call(gather_kernel, out_shape=(jax.ShapeDtypeStruct((NY, NZ, NX...  60.9 us
    unnamed x7, local copies, waits for them, and re-layouts  9.53 us
    dot_general x1, matrix products, shards(): lax.dot_general(f_all, u_all, (((0,), (0,)), ((), ())), preferred_element...  3.61 us

profile of v2, /device:TPU:32, one launch (start us, length us, event | category | flops | bytes accessed | tf_op | source)
XLA Modules:
  0.0 168.5 jit_solution(16754001584585818002)
XLA Ops:
  0.6 60.9 %shard_map.67 = (bf16[4,8,4,16,512]{4,3,2,1,0:T(8,128)(2,1)}, bf16[4,8,64,512]{3,2,1,0:T(8,128)(2,1)}, f32[512,512]{1,0:T(8,128)}) custom-call(bf16[128,4096]{1,0:T(8,128)(2,1)} %features.1, bf16[128,1024]{1,0:T(8,128)(2,1)} %upstream.1, f32[512,512]{1,0:T(8,128)} %bitcast.7), custom_call_target="tpu_custom_call" | custom-call | tf_op jit(solution)/shard_map/pallas_call | solution.py:270
  61.5 0.0 copy-start
  61.5 0.0 copy-start.1
  61.5 3.6 %fusion.partial = f32[512,512]{1,0:T(8,128)S(1)} fusion(bf16[2048,512]{1,0:T(8,128)(2,1)} %bitcast.8, bf16[2048,512]{1,0:T(8,128)(2,1)} %bitcast.9), kind=kOutput, calls=%fused_computation | convolution fusion | flops 1073741824 | bytes 5242880 | tf_op jit(solution)/shard_map/dot_general | solution.py:651
  65.1 0.0 copy-done
  65.2 0.0 copy-done.1
  65.2 93.8 %shard_map.68 = (bf16[4096,1024]{1,0:T(8,128)(2,1)}, f32[512,512]{1,0:T(8,128)S(1)}, f32[128,1024]{1,0:T(8,128)S(1)}) custom-call(f32[512,512]{1,0:T(8,128)S(1)} %fusion.partial, f32[512,512]{1,0:T(8,128)S(1)} %copy-done, f32[128,1024]{1,0:T(8,128)S(1)} %copy-done.1), custom_call_target="tpu_custom_call" | custom-call | tf_op jit(solution)/shard_map/pallas_call | solution.py:618
  159.0 1.0 copy.10
  160.0 0.8 copy.11
  160.8 7.8 %copy.12 = bf16[4096,1024]{1,0:T(8,128)(2,1)} copy(bf16[4096,1024]{1,0:T(8,128)(2,1)} %get-tuple-element.20) | data formatting | bytes 16777216
Async XLA Ops:
  61.5 3.6 %copy-start = (f32[512,512]{1,0:T(8,128)S(1)}, f32[512,512]{1,0:T(8,128)}, u32[]{:S(2)}) copy-start(f32[512,512]{1,0:T(8,128)} %get-tuple-element.11.stats) | copy-start | bytes 3145732
  61.5 3.6 %copy-start.1 = (f32[128,1024]{1,0:T(8,128)S(1)}, f32[128,1024]{1,0:T(8,128)}, u32[]{:S(2)}) copy-start(f32[128,1024]{1,0:T(8,128)} %accum.1) | copy-start | bytes 1572868

commit v3 on v2

--- a/solution.py
+++ b/solution.py
@@ -47,244 +47,194 @@
     )
 
 
-Z_ORDER = (0, 1, 7, 2, 6, 3, 5, 4)
-
-
-def gather_kernel(
-    features, upstream, stats, f_out, u_out, stat_out, f_y, stat_send, stat_recv,
+def gather_block(
+    features, upstream, partial, f_all, u_all, f_y,
     fy_send, fy_recv, fz_send, fz_recv, fx_send, fx_recv,
-    uz_send, uz_recv, uy_send, uy_recv, local_sem,
+    uz_send, uz_recv, uy_send, uy_recv, keep_sem, send_stats,
 ):
     x, y, z, core = place()
-    partners = [device(wrap(x + 1, NX), y, z, core), device(wrap(x - 1, NX), y, z, core)]
-    partners += [device(x, wrap(y + a, NY), z, core) for a in range(1, NY)]
-    partners += [device(x, y, wrap(z + d, NZ), c) for d in range(1, NZ) for c in range(NC)]
-    partners += [device(x, y, z, 1 - core)]
-    greet(partners)
-
+    up, down, far_y = wrap(y + 1, NY), wrap(y - 1, NY), wrap(y + 2, NY)
+    right, left, far_x = wrap(x + 1, NX), wrap(x - 1, NX), wrap(x + 2, NX)
+    here = device(x, y, z, core)
     sends = []
 
     def go(copy):
         copy.start()
         sends.append(copy)
 
-    up, down = wrap(y + 1, NY), wrap(y - 1, NY)
-    right, left = wrap(x + 1, NX), wrap(x - 1, NX)
-
-    swapped = z % NC != core
-
-    def stat_rows(i):
-        return pl.ds(128 * i, 128), pl.ds(128 * i, BLOCK - 128 * i)
-
-    stat_copies = [
-        remote(
-            stats.at[stat_rows(i)],
-            stat_out.at[stat_rows(i)],
-            stat_send.at[i],
-            stat_recv.at[i],
-            device(x, y, z + 1 - 2 * (z % NC), 1 - core),
-        )
-        for i in range(4)
-    ]
-    stat_keep = pltpu.make_async_copy(stats, stat_out, local_sem.at[3])
+    def origin(d):
+        return wrap(z - d, NZ)
 
     my_tokens = pl.ds(pl.multiple_of(64 * core + 16 * x, 16), 16)
 
     def f_cols(row):
         return features.at[my_tokens, pl.ds(pl.multiple_of(row * 1024, 1024), 1024)]
 
-    for a in (2, 1, 3):
-        row = wrap(y + a, NY)
-        go(remote(f_cols(row), f_y.at[y], fy_send.at[a], fy_recv.at[a], device(x, row, z, core)))
-    f_own = pltpu.make_async_copy(f_cols(y), f_y.at[y], local_sem.at[0])
-    f_own.start()
+    def fy_start():
+        for a in (2, 1, 3):
+            row = wrap(y + a, NY)
+            go(remote(f_cols(row), f_y.at[y], fy_send.at[a], fy_recv.at[a], device(x, row, z, core)))
+
+    f_own = pltpu.make_async_copy(f_cols(y), f_y.at[y], keep_sem.at[0])
+
+    def fy_wait():
+        f_own.wait()
+        for a in (1, 3, 2):
+            into = f_y.at[wrap(y - a, NY)]
+            remote(into, into, fy_send.at[a], fy_recv.at[a], here).wait_recv()
+
+    def f_half(row):
+        return f_y.at[:, :, pl.ds(pl.multiple_of(row // 4 * BLOCK, BLOCK), BLOCK)]
+
+    f_keep = pltpu.make_async_copy(f_half(z), f_all.at[z, :, x], keep_sem.at[1])
+
+    def fz_start(*distances):
+        for d in distances:
+            row = wrap(z + d, NZ)
+            go(
+                remote(
+                    f_half(row), f_all.at[z, :, x], fz_send.at[d], fz_recv.at[d], device(x, y, row, core)
+                )
+            )
 
     parity = wrap(core - z % NC, NC)
+    on_chip = parity == 0
 
     def u_tile(token_half, row):
         column = pl.multiple_of((row // 2) % 2 * BLOCK, BLOCK)
         return upstream.at[pl.ds(64 * token_half, 64), pl.ds(column, BLOCK)]
 
-    here = parity == 0
-    for j in (2, 1, 3, 0):
+    u_keep = pltpu.make_async_copy(u_tile(core, z), u_all.at[z, y], keep_sem.at[2])
+
+    def u_remote(j, c):
         d = 2 * j + parity
         row = wrap(z + d, NZ)
+        return remote(
+            u_tile(c, row), u_all.at[z, y], uz_send.at[j, c], uz_recv.at[d], device(x, y, row, c)
+        )
+
+    def uz_start(*steps):
+        for j in steps:
+            for c in range(NC):
+                copy = u_remote(j, c)
+                if j == 0:
+                    pl.when(jnp.logical_not(on_chip & (core == c)))(copy.start)
+                else:
+                    go(copy)
+
+    def uz_finish():
         for c in range(NC):
-            copy = remote(
-                u_tile(c, row), u_out.at[y, z], uz_send.at[j, c], uz_recv.at[d], device(x, y, row, c)
-            )
-            if j == 0:
-                mine = here & (core == c)
-
-                @pl.when(mine)
-                def _():
-                    pltpu.make_async_copy(u_tile(c, z), u_out.at[y, z], local_sem.at[1]).start()
-
-                @pl.when(jnp.logical_not(mine))
-                def _():
-                    copy.start()
-            else:
-                go(copy)
-
-    @pl.when(swapped)
-    def _():
-        for copy in stat_copies:
-            copy.start()
-
-    @pl.when(jnp.logical_not(swapped))
-    def _():
-        stat_keep.start()
-
-    f_own.wait()
-    for a in (1, 3, 2):
-        origin = wrap(y - a, NY)
-        remote(f_cols(y), f_y.at[origin], fy_send.at[a], fy_recv.at[a], device(x, y, z, core)).wait_recv()
-
-    def f_half(row):
-        return f_y.at[:, :, pl.ds(pl.multiple_of(row // 4 * BLOCK, BLOCK), BLOCK)]
-
-    for d in (4, 3, 5, 2, 6, 1, 7):
-        row = wrap(z + d, NZ)
-        go(
-            remote(
-                f_half(row), f_out.at[:, z, x], fz_send.at[d], fz_recv.at[d], device(x, y, row, core)
-            )
-        )
-    f_keep = pltpu.make_async_copy(f_half(z), f_out.at[:, z, x], local_sem.at[2])
-    f_keep.start()
-
-    def u_part(row, origin, part):
-        ref = u_out.at[row, origin]
+            pl.when(jnp.logical_not(on_chip & (core == c)))(u_remote(0, c).wait_send)
+
+    def u_part(d, row, part):
+        ref = u_all.at[origin(d), row]
         return ref if part is None else ref.at[pl.ds(32 * part, 32), :]
 
-    def send_u(origin, d, slot, row, part, forward_to):
-        ref = u_part(row, origin, part)
-        go(remote(ref, ref, uy_send.at[d, slot], uy_recv.at[d, slot], device(x, forward_to, z, core)))
-
-    def wait_u(origin, d, slot, row, part):
-        ref = u_part(row, origin, part)
-        remote(ref, ref, uy_send.at[d, slot], uy_recv.at[d, slot], device(x, up, z, core)).wait_recv()
-
-    def f_part(column, origin, part):
-        return f_out.at[:, origin, column] if part is None else f_out.at[pl.ds(2 * part, 2), origin, column]
-
-    def send_f(origin, d, slot, column, part, forward_to):
-        ref = f_part(column, origin, part)
-        go(remote(ref, ref, fx_send.at[d, slot], fx_recv.at[d, slot], device(forward_to, y, z, core)))
-
-    def wait_f(origin, d, slot, column, part):
-        ref = f_part(column, origin, part)
-        remote(ref, ref, fx_send.at[d, slot], fx_recv.at[d, slot], device(right, y, z, core)).wait_recv()
-
-    def u_first(d):
-        origin = wrap(z - d, NZ)
-        ref = u_out.at[y, origin]
-        arrived = remote(ref, ref, uz_send.at[0, 0], uz_recv.at[d], device(x, y, z, core))
+    def u_copy(d, slot, row, part, target):
+        ref = u_part(d, row, part)
+        return remote(ref, ref, uy_send.at[d, slot], uy_recv.at[d, slot], device(x, target, z, core))
+
+    def f_part(d, column, part):
+        if part is None:
+            return f_all.at[origin(d), :, column]
+        return f_all.at[origin(d), pl.ds(2 * part, 2), column]
+
+    def f_copy(d, slot, column, part, target):
+        ref = f_part(d, column, part)
+        return remote(ref, ref, fx_send.at[d, slot], fx_recv.at[d, slot], device(target, y, z, core))
+
+    def u1(d):
+        ref = u_all.at[origin(d), y]
+        arrived = remote(ref, ref, uz_send.at[0, 0], uz_recv.at[d], here)
         if d == 0:
-            mine = z % NC == core
-
-            @pl.when(mine)
-            def _():
-                pltpu.make_async_copy(ref, ref, local_sem.at[1]).wait()
-
-            @pl.when(jnp.logical_not(mine))
-            def _():
-                arrived.wait_recv()
+            pl.when(on_chip)(u_keep.wait)
+            pl.when(jnp.logical_not(on_chip))(arrived.wait_recv)
         else:
             arrived.wait_recv()
-        send_u(origin, d, 0, y, None, up)
-        send_u(origin, d, 1, y, None, down)
-
-    def u_second(d):
-        origin = wrap(z - d, NZ)
-        wait_u(origin, d, 0, down, None)
-        send_u(origin, d, 2, down, 0, up)
-        wait_u(origin, d, 1, up, None)
-        send_u(origin, d, 3, up, 1, down)
-
-    def u_last(d):
-        origin = wrap(z - d, NZ)
-        far = wrap(y + 2, NY)
-        wait_u(origin, d, 2, far, 0)
-        wait_u(origin, d, 3, far, 1)
-
-    def f_first(d):
-        origin = wrap(z - d, NZ)
-        ref = f_out.at[:, origin, x]
+        go(u_copy(d, 0, y, None, up))
+        go(u_copy(d, 1, y, None, down))
+
+    def u2(d):
+        u_copy(d, 0, down, None, up).wait_recv()
+        go(u_copy(d, 2, down, 0, up))
+        u_copy(d, 1, up, None, down).wait_recv()
+        go(u_copy(d, 3, up, 1, down))
+
+    def f1(d):
+        ref = f_all.at[origin(d), :, x]
         if d == 0:
             f_keep.wait()
         else:
-            remote(ref, ref, fz_send.at[d], fz_recv.at[d], device(x, y, z, core)).wait_recv()
-        send_f(origin, d, 0, x, None, right)
-        send_f(origin, d, 1, x, None, left)
-
-    def f_second(d):
-        origin = wrap(z - d, NZ)
-        wait_f(origin, d, 0, left, None)
-        send_f(origin, d, 2, left, 0, right)
-        wait_f(origin, d, 1, right, None)
-        send_f(origin, d, 3, right, 1, left)
-
-    def f_last(d):
-        origin = wrap(z - d, NZ)
-        far = wrap(x + 2, NX)
-        wait_f(origin, d, 2, far, 0)
-        wait_f(origin, d, 3, far, 1)
-
-    f_first(0)
-    for step in range(NZ + 3):
-        if step < NZ:
-            u_first(Z_ORDER[step])
-        if 1 <= step <= NZ - 1:
-            f_first(Z_ORDER[step])
-        if 1 <= step <= NZ:
-            u_second(Z_ORDER[step - 1])
-        if 2 <= step <= NZ + 1:
-            f_second(Z_ORDER[step - 2])
-        if 2 <= step <= NZ + 1:
-            u_last(Z_ORDER[step - 2])
-        if 3 <= step <= NZ + 2:
-            f_last(Z_ORDER[step - 3])
-
-    @pl.when(swapped)
-    def _():
-        for copy in stat_copies:
-            copy.wait()
-
-    @pl.when(jnp.logical_not(swapped))
-    def _():
-        stat_keep.wait()
-
-    for copy in sends:
-        copy.wait_send()
-    for c in range(NC):
-        @pl.when(jnp.logical_not(here & (core == c)))
-        def _():
-            remote(
-                u_tile(c, z), u_out.at[y, z], uz_send.at[0, c], uz_recv.at[0], device(x, y, z, 1 - core)
-            ).wait_send()
-
-
-def gather_inputs(features, upstream, stats):
-    dma = pltpu.SemaphoreType.DMA
-    f_all, u_all, stat = pl.pallas_call(
-        gather_kernel,
-        out_shape=(
-            jax.ShapeDtypeStruct((NY, NZ, NX, 16, BLOCK), jnp.bfloat16),
-            jax.ShapeDtypeStruct((NY, NZ, 64, BLOCK), jnp.bfloat16),
-            jax.ShapeDtypeStruct((BLOCK, BLOCK), jnp.float32),
-        ),
-        in_specs=[pl.BlockSpec(memory_space=pl.ANY)] * 3,
-        out_specs=(pl.BlockSpec(memory_space=pl.ANY),) * 3,
-        scratch_shapes=[
-            pltpu.VMEM((NY, 16, 1024), jnp.bfloat16),
-            dma((4,)), dma((4,)),
-            dma((NY,)), dma((NY,)), dma((NZ,)), dma((NZ,)), dma((NZ, 4)), dma((NZ, 4)),
-            dma((4, NC)), dma((NZ,)), dma((NZ, 4)), dma((NZ, 4)), dma((4,)),
-        ],
-        compiler_params=pltpu.CompilerParams(collective_id=0, has_side_effects=True),
-    )(features, upstream, stats)
-    return f_all.reshape(-1, BLOCK), u_all.reshape(-1, BLOCK), stat
+            remote(ref, ref, fz_send.at[d], fz_recv.at[d], here).wait_recv()
+        go(f_copy(d, 0, x, None, right))
+        go(f_copy(d, 1, x, None, left))
+
+    def f2(d):
+        f_copy(d, 0, left, None, right).wait_recv()
+        go(f_copy(d, 2, left, 0, right))
+        f_copy(d, 1, right, None, left).wait_recv()
+        go(f_copy(d, 3, right, 1, left))
+
+    def add(d):
+        for part in range(2):
+            u_copy(d, 2 + part, far_y, part, up).wait_recv()
+            f_copy(d, 2 + part, far_x, part, right).wait_recv()
+        term = lax.dot_general(
+            f_all[origin(d)].reshape(256, BLOCK),
+            u_all[origin(d)].reshape(256, BLOCK),
+            (((0,), (0,)), ((), ())),
+            preferred_element_type=jnp.float32,
+        )
+        partial[...] = term if d == 0 else partial[...] + term
+
+    fy_start()
+    f_own.start()
+    uz_start(0, 3)
+    pl.when(on_chip)(u_keep.start)
+    fy_wait()
+    fz_start(1, 7)
+    f_keep.start()
+    u1(0)
+    f1(0)
+    for d in (1, 7):
+        u1(d)
+    for d in (1, 7):
+        f1(d)
+    fz_start(2, 6)
+    u1(6)
+    uz_start(1, 2)
+    for d in (0, 1, 7):
+        u2(d)
+        f2(d)
+    for d in (2, 6):
+        f1(d)
+    fz_start(3, 5)
+    u2(6)
+    f2(2)
+    for d in (2, 3, 5, 4):
+        u1(d)
+    fz_start(4)
+    send_stats()
+    add(0)
+    f2(6)
+    u2(2)
+    u2(3)
+    add(1)
+    f1(3)
+    f1(5)
+    u2(5)
+    u2(4)
+    add(7)
+    f2(3)
+    f2(5)
+    f1(4)
+    add(6)
+    add(2)
+    f2(4)
+    add(3)
+    add(5)
+    add(4)
+    return sends, uz_finish
 
 
 def spread_plan():
@@ -387,10 +337,11 @@
 
 
 def step_kernel(
-    partial, stats, accum, out, new_stat, new_accum,
-    partial_other, block, stat, iterate, coupled, root_other, pieces, precond, sums,
+    features, upstream, stats, accum, out, new_stat, new_accum,
+    f_all, u_all, f_y, accum_here, stat_other, partial, partial_other, block, stat, iterate, coupled, root_other, pieces, precond, sums,
     other_block, shard, mp_sums, y_sums, z_sums, mp_total, y_total,
-    core_sem, piece_send, piece_recv, stat_sem, root_sem,
+    fy_send, fy_recv, fz_send, fz_recv, fx_send, fx_recv, uz_send, uz_recv, uy_send, uy_recv, keep_sem,
+    load_sem, stats_send, stats_recv, core_sem, piece_send, piece_recv, stat_sem, root_sem,
     mp_send, mp_recv, ys_send, ys_recv, zs_send, zs_recv, swap_sem, send_sem, recv_sem, local_sem,
 ):
     x, y, z, core = place()
@@ -404,14 +355,48 @@
     right_side = core == 1
     other_core = device(x, y, z, 1 - core)
     swap_peer = device(x, y, z + 1 - 2 * (z % NC), 1 - core)
-    greet(mp_peers + y_peers + z_peers + [swap_peer])
+    across = [device(x, y, wrap(z + j, NZ), 1 - core) for j in range(1, NZ)]
+    greet(mp_peers + y_peers + z_peers + across)
+    accum_load = pltpu.make_async_copy(accum, accum_here, load_sem.at[0])
+    stat_load = pltpu.make_async_copy(stats, stat, load_sem.at[1])
+    accum_load.start()
+    pl.when(straight)(stat_load.start)
+
+    stat_copies = []
+    for i in range(4):
+        at = pl.ds(128 * i, 128), pl.ds(128 * i, BLOCK - 128 * i)
+        stat_copies.append(
+            remote(stats.at[at], stat_other.at[at], stats_send.at[i], stats_recv.at[i], swap_peer)
+        )
+
+    def send_stats():
+        for copy in stat_copies:
+            pl.when(swapped)(copy.start)
+
+    gather_sends, gather_finish = gather_block(
+        features, upstream, partial, f_all, u_all, f_y,
+        fy_send, fy_recv, fz_send, fz_recv, fx_send, fx_recv,
+        uz_send, uz_recv, uy_send, uy_recv, keep_sem, send_stats,
+    )
 
     exchange = remote(partial, partial_other, core_sem.at[0], core_sem.at[1], other_core)
     exchange.start()
-    shape = (BLOCK, BLOCK)
-    below = lax.broadcasted_iota(jnp.int32, shape, 0) // 128 > lax.broadcasted_iota(jnp.int32, shape, 1) // 128
-    kept = stats[...]
-    stat[...] = jnp.where(below & swapped, kept.T, kept)
+
+    @pl.when(swapped)
+    def _():
+        for copy in stat_copies:
+            copy.wait()
+        for i in range(1, 4):
+            for j in range(i):
+                stat_other[128 * i : 128 * i + 128, 128 * j : 128 * j + 128] = stat_other[
+                    128 * j : 128 * j + 128, 128 * i : 128 * i + 128
+                ].T
+        stat[...] = stat_other[...]
+
+    @pl.when(straight)
+    def _():
+        stat_load.wait()
+
     exchange.wait()
     both = partial[...] + partial_other[...]
     block[...] = both
@@ -480,11 +465,12 @@
         def _():
             remote(pieces.at[c], pieces.at[c], piece_send.at[1], piece_recv.at[c], other_core).wait_recv()
 
+    accum_load.wait()
     adagrad_total = jnp.zeros((1, 1), jnp.float32)
     for c in range(2):
         columns = slice(c * BLOCK, (c + 1) * BLOCK)
         squares = pieces[c] * pieces[c]
-        grown = accum[:, columns] + squares
+        grown = accum_here[:, columns] + squares
         new_accum[:, columns] = grown
         adagrad_total = adagrad_total + jnp.sum(squares / grown, keepdims=True)
 
@@ -595,8 +581,9 @@
         remote(here, here, send_sem.at[index], recv_sem.at[index], swap_peer).wait_recv()
         for one in onward:
             send(*one)
-    for copy in sent + sent_mp + sent_y + sent_z:
+    for copy in gather_sends + sent + sent_mp + sent_y + sent_z:
         copy.wait_send()
+    gather_finish()
     whole.wait()
 
     @pl.when(swapped)
@@ -609,7 +596,7 @@
             copy.wait_send()
 
 
-def take_step(partial, stats, accum):
+def take_step(features, upstream, stats, accum):
     dma = pltpu.SemaphoreType.DMA
     tile = (8, 128)
     count = len(spread_schedule()[1])
@@ -618,14 +605,18 @@
     return pl.pallas_call(
         step_kernel,
         out_shape=(
-            jax.ShapeDtypeStruct((NY * NZ * 128, 1024), jnp.bfloat16),
-            jax.ShapeDtypeStruct((BLOCK, BLOCK), jnp.float32),
-            jax.ShapeDtypeStruct(accum.shape, jnp.float32),
+            pltpu.VMEM((NY * NZ * 128, 1024), jnp.bfloat16),
+            pltpu.VMEM((BLOCK, BLOCK), jnp.float32),
+            pltpu.VMEM(accum.shape, jnp.float32),
         ),
-        in_specs=[vmem] * 3,
-        out_specs=(pl.BlockSpec(memory_space=pl.ANY), vmem, vmem),
+        in_specs=[pl.BlockSpec(memory_space=pltpu.HBM)] * 4,
+        out_specs=(vmem, vmem, vmem),
         scratch_shapes=[
-            square, square, square, square, square, square,
+            pltpu.VMEM((NZ, NY, NX, 16, BLOCK), jnp.bfloat16),
+            pltpu.VMEM((NZ, NY, 64, BLOCK), jnp.bfloat16),
+            pltpu.VMEM((NY, 16, 1024), jnp.bfloat16),
+            pltpu.VMEM(accum.shape, jnp.float32),
+            square, square, square, square, square, square, square, square,
             pltpu.VMEM((2, 128, BLOCK), jnp.float32),
             pltpu.VMEM((HALF, BLOCK), jnp.float32),
             pltpu.VMEM(tile, jnp.float32),
@@ -636,22 +627,20 @@
             pltpu.VMEM((NZ, *tile), jnp.float32),
             pltpu.VMEM(tile, jnp.float32),
             pltpu.VMEM(tile, jnp.float32),
-            dma((2,)), dma((4,)), dma((2,)), dma((2,)), dma((2,)),
+            dma((NY,)), dma((NY,)), dma((NZ,)), dma((NZ,)), dma((NZ, 4)), dma((NZ, 4)),
+            dma((4, NC)), dma((NZ,)), dma((NZ, 4)), dma((NZ, 4)), dma((3,)),
+            dma((2,)), dma((4,)), dma((4,)), dma((2,)), dma((4,)), dma((2,)), dma((2,)), dma((2,)),
             dma((NX * NC,)), dma((NX * NC,)), dma((NY,)), dma((NY,)), dma((NZ,)), dma((NZ,)),
             dma((2,)), dma((count,)), dma((count,)), dma((1,)),
         ],
         compiler_params=pltpu.CompilerParams(
-            collective_id=1, has_side_effects=True, vmem_limit_bytes=48 * 2**20
+            collective_id=0, has_side_effects=True, vmem_limit_bytes=50 * 2**20
         ),
-    )(partial, stats, accum)
+    )(features, upstream, stats, accum)
 
 
 def shards(features, upstream, stats, accum):
-    f_all, u_all, stat = gather_inputs(features, upstream, stats[0, 0])
-    partial = lax.dot_general(
-        f_all, u_all, (((0,), (0,)), ((), ())), preferred_element_type=jnp.float32
-    )
-    update, new_stat, new_accum = take_step(partial, stat, accum)
+    update, new_stat, new_accum = take_step(features, upstream, stats[0, 0], accum)
     return (new_stat[None, None], new_accum, update)
 
 

time: 169 us -> 147 us (0.87)
  Pallas kernels: 155 us -> 141 us
  local copies, waits for them, and re-layouts: 9.53 us -> 5.16 us
  matrix products: 3.61 us -> 0 us
    pallas_call x2 -> x1, Pallas kernels: 155 us -> 141 us  [take_step(): pl.pallas_call(step_kernel, out_shape=(pltpu.VMEM((NY * NZ * 128, 1024),...]
    unnamed x7 -> x3, local copies, waits for them, and re-layouts: 9.53 us -> 5.16 us
    dot_general x1 -> x0, matrix products: 3.61 us -> none  [shards(): lax.dot_general(f_all, u_all, (((0,), (0,)), ((), ())), preferred_element...]
where the time goes in v3:
time: 147 us
  Pallas kernels  141 us (96%)
  local copies, waits for them, and re-layouts  5.16 us (4%)
    pallas_call x1, Pallas kernels, take_step(): pl.pallas_call(step_kernel, out_shape=(pltpu.VMEM((NY * NZ * 128, 1024),...  141 us
    unnamed x3, local copies, waits for them, and re-layouts  5.16 us

profile of v3, /device:TPU:32, one launch (start us, length us, event | category | flops | bytes accessed | tf_op | source)
XLA Modules:
  0.0 146.9 jit_solution(14438733134983420223)
XLA Ops:
  0.6 141.1 %shard_map.67 = (bf16[4096,1024]{1,0:T(8,128)(2,1)S(1)}, f32[512,512]{1,0:T(8,128)S(1)}, f32[128,1024]{1,0:T(8,128)S(1)}) custom-call(bf16[128,4096]{1,0:T(8,128)(2,1)} %features.1, bf16[128,1024]{1,0:T(8,128)(2,1)} %upstream.1, f32[512,512]{1,0:T(8,128)} %bitcast.3, f32[128,1024]{1,0:T(8,128)} %accum.1), custom_call_target="tpu_custom_call" | custom-call | tf_op jit(solution)/shard_map/pallas_call | solution.py:605
  141.7 1.0 copy.10
  142.7 0.8 copy.11
  143.5 3.4 %copy.12 = bf16[4096,1024]{1,0:T(8,128)(2,1)} copy(bf16[4096,1024]{1,0:T(8,128)(2,1)S(1)} %get-tuple-element.11) | data formatting | bytes 16777216

commit v4 on v3

--- a/solution.py
+++ b/solution.py
@@ -88,14 +88,33 @@
 
     f_keep = pltpu.make_async_copy(f_half(z), f_all.at[z, :, x], keep_sem.at[1])
 
-    def fz_start(*distances):
-        for d in distances:
-            row = wrap(z + d, NZ)
-            go(
-                remote(
-                    f_half(row), f_all.at[z, :, x], fz_send.at[d], fz_recv.at[d], device(x, y, row, core)
-                )
-            )
+    spot = z % 4
+    maybe = []
+
+    def go_if(condition, copy):
+        pl.when(condition)(copy.start)
+        maybe.append((condition, copy))
+
+    def fz_copy(source, slot, d, row):
+        into = f_all.at[wrap(row - d, NZ), :, x]
+        return remote(source, into, fz_send.at[slot], fz_recv.at[d], device(x, y, row, core))
+
+    def fz_start():
+        above, below, two_up, two_down = (wrap(z + step, NZ) for step in (1, -1, 2, -2))
+        go(fz_copy(f_half(above), 0, 1, above))
+        go(fz_copy(f_half(below), 8, 7, below))
+        go_if(spot == 1, fz_copy(f_half(two_down), 9, 6, two_down))
+        go_if(spot == 2, fz_copy(f_half(two_up), 9, 2, two_up))
+
+    def fz_pass(d):
+        ref = f_all.at[origin(d), :, x]
+        above, below = wrap(z + 1, NZ), wrap(z - 1, NZ)
+        rising = {1: spot < 3, 2: spot < 3, 3: (spot == 1) | (spot == 2), 4: spot == 2}
+        falling = {7: spot > 0, 6: spot > 0, 5: (spot == 1) | (spot == 2), 4: spot == 1}
+        if d in rising:
+            go_if(rising[d], fz_copy(ref, d, d + 1, above))
+        if d in falling:
+            go_if(falling[d], fz_copy(ref, d, d - 1, below))
 
     parity = wrap(core - z % NC, NC)
     on_chip = parity == 0
@@ -166,6 +185,7 @@
             f_keep.wait()
         else:
             remote(ref, ref, fz_send.at[d], fz_recv.at[d], here).wait_recv()
+            fz_pass(d)
         go(f_copy(d, 0, x, None, right))
         go(f_copy(d, 1, x, None, left))
 
@@ -192,49 +212,51 @@
     uz_start(0, 3)
     pl.when(on_chip)(u_keep.start)
     fy_wait()
-    fz_start(1, 7)
+    fz_start()
     f_keep.start()
     u1(0)
     f1(0)
-    for d in (1, 7):
-        u1(d)
-    for d in (1, 7):
-        f1(d)
-    fz_start(2, 6)
+    uz_start(1)
+    u1(1)
+    u1(7)
+    f1(1)
+    f1(7)
     u1(6)
-    uz_start(1, 2)
+    uz_start(2)
     for d in (0, 1, 7):
         u2(d)
         f2(d)
-    for d in (2, 6):
-        f1(d)
-    fz_start(3, 5)
+    f1(2)
+    f1(6)
+    u1(2)
+    u1(3)
     u2(6)
     f2(2)
-    for d in (2, 3, 5, 4):
-        u1(d)
-    fz_start(4)
+    f2(6)
     send_stats()
-    add(0)
-    f2(6)
+    f1(3)
+    f1(5)
     u2(2)
     u2(3)
+    u1(5)
+    u1(4)
+    add(0)
+    f1(4)
+    f2(3)
+    f2(5)
     add(1)
-    f1(3)
-    f1(5)
     u2(5)
     u2(4)
-    add(7)
-    f2(3)
-    f2(5)
-    f1(4)
-    add(6)
-    add(2)
     f2(4)
-    add(3)
-    add(5)
-    add(4)
-    return sends, uz_finish
+    for d in (7, 6, 2, 3, 5, 4):
+        add(d)
+
+    def finish():
+        uz_finish()
+        for condition, copy in maybe:
+            pl.when(condition)(copy.wait_send)
+
+    return sends, finish
 
 
 def spread_plan():
@@ -310,11 +332,17 @@
     return dot(first[0], second[0]) + (dot(first[0], second[1]) + dot(first[1], second[0]))
 
 
+def symmetric_product(first, second):
+    left = product(first, [part[:, :HALF] for part in second])
+    last = product([part[HALF:] for part in first], [part[:, HALF:] for part in second])
+    return jnp.concatenate([left, jnp.concatenate([left[HALF:].T, last], 0)], 1)
+
+
 def newton_root(stat, iterate, coupled):
     def advance(now, now_parts):
-        change = split((product(now_parts, now_parts) - 10.0 * now) * (1 / 16))
-        once = (25 / 16) * now + product(change, now_parts)
-        return (25 / 16) * once + product(change, split(once))
+        change = split((symmetric_product(now_parts, now_parts) - 10.0 * now) * (1 / 16))
+        once = (25 / 16) * now + symmetric_product(change, now_parts)
+        return (25 / 16) * once + symmetric_product(change, split(once))
 
     start = stat[...]
     factor = 2.5 / jnp.sqrt(jnp.sum(start * start, keepdims=True))
@@ -327,13 +355,13 @@
     def body(_, carry):
         now, root = coupled[...], iterate[...]
         now_parts = split(now)
-        iterate[...] = 1.25 * root - 0.25 * product(split(root), now_parts)
+        iterate[...] = 1.25 * root - 0.25 * symmetric_product(split(root), now_parts)
         coupled[...] = advance(now, now_parts)
         return carry
 
     lax.fori_loop(0, ITERS - 2, body, 0)
     root = iterate[...]
-    iterate[...] = 1.25 * root - 0.25 * product(split(root), split(coupled[...]))
+    iterate[...] = 1.25 * root - 0.25 * symmetric_product(split(root), split(coupled[...]))
 
 
 def step_kernel(
@@ -426,7 +454,7 @@
     turned = both.T
     first = jnp.where(left_side, both, turned)
     second = jnp.where(left_side, turned, both)
-    stat[...] = stat[...] + product(split(first), split(second))
+    stat[...] = stat[...] + symmetric_product(split(first), split(second))
     stat_back = remote(stat, new_stat, stat_sem.at[0], stat_sem.at[1], swap_peer)
 
     @pl.when(swapped)
@@ -627,7 +655,7 @@
             pltpu.VMEM((NZ, *tile), jnp.float32),
             pltpu.VMEM(tile, jnp.float32),
             pltpu.VMEM(tile, jnp.float32),
-            dma((NY,)), dma((NY,)), dma((NZ,)), dma((NZ,)), dma((NZ, 4)), dma((NZ, 4)),
+            dma((NY,)), dma((NY,)), dma((NZ + 2,)), dma((NZ,)), dma((NZ, 4)), dma((NZ, 4)),
             dma((4, NC)), dma((NZ,)), dma((NZ, 4)), dma((NZ, 4)), dma((3,)),
             dma((2,)), dma((4,)), dma((4,)), dma((2,)), dma((4,)), dma((2,)), dma((2,)), dma((2,)),
             dma((NX * NC,)), dma((NX * NC,)), dma((NY,)), dma((NY,)), dma((NZ,)), dma((NZ,)),

time: 147 us -> 144 us (0.980)
  Pallas kernels: 141 us -> 137 us
    pallas_call x1, Pallas kernels: 141 us -> 137 us  [take_step(): pl.pallas_call(step_kernel, out_shape=(pltpu.VMEM((NY * NZ * 128, 1024),...]
where the time goes in v4:
time: 144 us; the launch traced here: 143 us
  Pallas kernels  137 us (95%)
  local copies, waits for them, and re-layouts  5.16 us (4%)
    pallas_call x1, Pallas kernels, take_step(): pl.pallas_call(step_kernel, out_shape=(pltpu.VMEM((NY * NZ * 128, 1024),...  137 us
    unnamed x3, local copies, waits for them, and re-layouts  5.16 us

profile of v4, /device:TPU:32, one launch (start us, length us, event | category | flops | bytes accessed | tf_op | source)
XLA Modules:
  0.0 143.3 jit_solution(3581810012662704847)
XLA Ops:
  0.6 137.5 %shard_map.67 = (bf16[4096,1024]{1,0:T(8,128)(2,1)S(1)}, f32[512,512]{1,0:T(8,128)S(1)}, f32[128,1024]{1,0:T(8,128)S(1)}) custom-call(bf16[128,4096]{1,0:T(8,128)(2,1)} %features.1, bf16[128,1024]{1,0:T(8,128)(2,1)} %upstream.1, f32[512,512]{1,0:T(8,128)} %bitcast.3, f32[128,1024]{1,0:T(8,128)} %accum.1), custom_call_target="tpu_custom_call" | custom-call | tf_op jit(solution)/shard_map/pallas_call | solution.py:633
  138.1 1.0 copy.10
  139.1 0.8 copy.11
  139.9 3.4 %copy.12 = bf16[4096,1024]{1,0:T(8,128)(2,1)} copy(bf16[4096,1024]{1,0:T(8,128)(2,1)S(1)} %get-tuple-element.11) | data formatting | bytes 16777216

commit v5 on v4

--- a/solution.py
+++ b/solution.py
@@ -209,14 +209,14 @@
 
     fy_start()
     f_own.start()
-    uz_start(0, 3)
+    uz_start(0, 3, 1)
     pl.when(on_chip)(u_keep.start)
     fy_wait()
     fz_start()
     f_keep.start()
+    send_stats()
     u1(0)
     f1(0)
-    uz_start(1)
     u1(1)
     u1(7)
     f1(1)
@@ -233,7 +233,6 @@
     u2(6)
     f2(2)
     f2(6)
-    send_stats()
     f1(3)
     f1(5)
     u2(2)
@@ -667,8 +666,35 @@
     )(features, upstream, stats, accum)
 
 
+def deliver_kernel(update, stat, accum, update_out, stat_out, accum_out, sems):
+    copies = []
+
+    def go(source, into):
+        copy = pltpu.make_async_copy(source, into, sems.at[len(copies)])
+        copy.start()
+        copies.append(copy)
+
+    for part in range(8):
+        rows = pl.ds(part * 512, 512)
+        go(update.at[rows, :], update_out.at[rows, :])
+    go(stat, stat_out)
+    go(accum, accum_out)
+    for copy in copies:
+        copy.wait()
+
+
+def deliver(update, stat, accum):
+    return pl.pallas_call(
+        deliver_kernel,
+        out_shape=tuple(jax.ShapeDtypeStruct(one.shape, one.dtype) for one in (update, stat, accum)),
+        in_specs=[pl.BlockSpec(memory_space=pl.ANY)] * 3,
+        out_specs=(pl.BlockSpec(memory_space=pltpu.HBM),) * 3,
+        scratch_shapes=[pltpu.SemaphoreType.DMA((10,))],
+    )(update, stat, accum)
+
+
 def shards(features, upstream, stats, accum):
-    update, new_stat, new_accum = take_step(features, upstream, stats[0, 0], accum)
+    update, new_stat, new_accum = deliver(*take_step(features, upstream, stats[0, 0], accum))
     return (new_stat[None, None], new_accum, update)
 
 

time: 144 us -> 446 us (3.10)
  Pallas kernels: 137 us -> 440 us
    pallas_call x0 -> x1, Pallas kernels: none -> 303 us  [deliver(): pl.pallas_call(deliver_kernel, out_shape=tuple((jax.ShapeDtypeStruct(one....]
where the time goes in v5:
time: 446 us
  Pallas kernels  440 us (99%)
  local copies, waits for them, and re-layouts  5.04 us (1%)
    pallas_call x1, Pallas kernels, deliver(): pl.pallas_call(deliver_kernel, out_shape=tuple((jax.ShapeDtypeStruct(one....  303 us
    pallas_call x1, Pallas kernels, take_step(): pl.pallas_call(step_kernel, out_shape=(pltpu.VMEM((NY * NZ * 128, 1024),...  137 us

profile of v5, /device:TPU:32, one launch (start us, length us, event | category | flops | bytes accessed | tf_op | source)
XLA Modules:
  0.0 445.9 jit_solution(6400662989950580718)
XLA Ops:
  0.6 137.3 %shard_map.67 = (bf16[4096,1024]{1,0:T(8,128)(2,1)S(1)}, f32[512,512]{1,0:T(8,128)S(1)}, f32[128,1024]{1,0:T(8,128)S(1)}) custom-call(bf16[128,4096]{1,0:T(8,128)(2,1)} %features.1, bf16[128,1024]{1,0:T(8,128)(2,1)} %upstream.1, f32[512,512]{1,0:T(8,128)} %bitcast.2, f32[128,1024]{1,0:T(8,128)} %accum.1), custom_call_target="tpu_custom_call" | custom-call | tf_op jit(solution)/shard_map/pallas_call | solution.py:632
  137.9 0.0 copy-start
  137.9 3.2 copy-done
  141.1 0.0 copy-start.1
  141.1 1.0 copy-done.1
  142.2 0.0 copy-start.2
  142.2 0.8 copy-done.2
  142.9 302.9 %shard_map.68 = (bf16[4096,1024]{1,0:T(8,128)(2,1)}, f32[512,512]{1,0:T(8,128)}, f32[128,1024]{1,0:T(8,128)}) custom-call(bf16[4096,1024]{1,0:T(8,128)(2,1)} %copy-done, f32[512,512]{1,0:T(8,128)} %copy-done.1, f32[128,1024]{1,0:T(8,128)} %copy-done.2), custom_call_target="tpu_custom_call" | custom-call | tf_op jit(solution)/shard_map/pallas_call | solution.py:687
Async XLA Ops:
  137.9 3.2 copy-start
  141.1 1.0 copy-start.1
  142.2 0.8 copy-start.2

commit v6 on v5

--- a/solution.py
+++ b/solution.py
@@ -209,14 +209,14 @@
 
     fy_start()
     f_own.start()
-    uz_start(0, 3, 1)
+    uz_start(0, 3)
     pl.when(on_chip)(u_keep.start)
     fy_wait()
     fz_start()
     f_keep.start()
-    send_stats()
     u1(0)
     f1(0)
+    uz_start(1)
     u1(1)
     u1(7)
     f1(1)
@@ -233,6 +233,7 @@
     u2(6)
     f2(2)
     f2(6)
+    send_stats()
     f1(3)
     f1(5)
     u2(2)
@@ -690,6 +691,7 @@
         in_specs=[pl.BlockSpec(memory_space=pl.ANY)] * 3,
         out_specs=(pl.BlockSpec(memory_space=pltpu.HBM),) * 3,
         scratch_shapes=[pltpu.SemaphoreType.DMA((10,))],
+        compiler_params=pltpu.CompilerParams(vmem_limit_bytes=2**20),
     )(update, stat, accum)
 
 

time: 446 us -> 143 us (0.32)
  Pallas kernels: 440 us -> 141 us
  local copies, waits for them, and re-layouts: 5.04 us -> 0 us
    pallas_call x1, Pallas kernels: 303 us -> 3.84 us  [deliver(): pl.pallas_call(deliver_kernel, out_shape=tuple((jax.ShapeDtypeStruct(one....]
    unnamed x6 -> x0, local copies, waits for them, and re-layouts: 5.04 us -> none
where the time goes in v6:
time: 143 us; the launch traced here: 142 us
  Pallas kernels  141 us (99%)
    pallas_call x1, Pallas kernels, take_step(): pl.pallas_call(step_kernel, out_shape=(pltpu.VMEM((NY * NZ * 128, 1024),...  137 us
    pallas_call x1, Pallas kernels, deliver(): pl.pallas_call(deliver_kernel, out_shape=tuple((jax.ShapeDtypeStruct(one....  3.84 us

profile of v6, /device:TPU:32, one launch (start us, length us, event | category | flops | bytes accessed | tf_op | source)
XLA Modules:
  0.0 142.0 jit_solution(12573306470837886333)
XLA Ops:
  0.6 137.5 %shard_map.67 = (bf16[4096,1024]{1,0:T(8,128)(2,1)S(1)}, f32[512,512]{1,0:T(8,128)S(1)}, f32[128,1024]{1,0:T(8,128)S(1)}) custom-call(bf16[128,4096]{1,0:T(8,128)(2,1)} %features.1, bf16[128,1024]{1,0:T(8,128)(2,1)} %upstream.1, f32[512,512]{1,0:T(8,128)} %bitcast.2, f32[128,1024]{1,0:T(8,128)} %accum.1), custom_call_target="tpu_custom_call" | custom-call | tf_op jit(solution)/shard_map/pallas_call | solution.py:633
  138.1 3.8 %shard_map.68 = (bf16[4096,1024]{1,0:T(8,128)(2,1)}, f32[512,512]{1,0:T(8,128)}, f32[128,1024]{1,0:T(8,128)}) custom-call(bf16[4096,1024]{1,0:T(8,128)(2,1)S(1)} %get-tuple-element.9.update, f32[512,512]{1,0:T(8,128)S(1)} %get-tuple-element.10.stat, f32[128,1024]{1,0:T(8,128)S(1)} %get-tuple-element.11.accum), custom_call_target="tpu_custom_call" | custom-call | tf_op jit(solution)/shard_map/pallas_call | solution.py:688
